TPU v7x, 32 devices: a whole 2x2x4 slice. The times are simulated.
32 devices in a mesh: dp: 8 (over z, y), ctx: 4 (over x, core).
Axes of the slice: x: 2, y: 2, z: 4, core: 2. Of those that a mesh axis runs over, the one named last changes fastest.
Arguments:
- tokens: bfloat16 [16, 2048, 960], P('dp', 'ctx'), may hold values from -6 to 6
- segments: int32 [16, 2048], P('dp', 'ctx'), may hold values from 0 to 34, as said below
- cotangent: float32 [16, 2048, 960], P('dp', 'ctx'), may hold values from -6 to 6
- attn_gain: bfloat16 [960], P('ctx'), may hold values from 0.5 to 1.5
- query_weight: bfloat16 [960, 960], P('dp', 'ctx'), may hold values from -0.1875 to 0.1875
- key_matrix: bfloat16 [960, 320], P('dp', 'ctx'), may hold values from -0.1875 to 0.1875
- value_matrix: bfloat16 [960, 320], P('dp', 'ctx'), may hold values from -0.1875 to 0.1875
- output_weight: bfloat16 [960, 960], P('dp', 'ctx'), may hold values from -1.25 to 1.25
- second_gain: bfloat16 [960], P('ctx'), may hold values from 0.5 to 1.5
- gate_weight: bfloat16 [960, 2560], P('dp', 'ctx'), may hold values from -0.1875 to 0.1875
- up_weight: bfloat16 [960, 2560], P('dp', 'ctx'), may hold values from -0.1875 to 0.1875
- down_weight: bfloat16 [2560, 960], P('dp', 'ctx'), may hold values from -0.125 to 0.125
Outputs:
- block_output: bfloat16 [16, 2048, 960], P('dp', 'ctx')
- input_grad: float32 [16, 2048, 960], P('dp', 'ctx')
- attn_gain_grad: float32 [960], P('ctx')
- query_grad: float32 [960, 960], P('dp', 'ctx')
- key_grad: float32 [960, 320], P('dp', 'ctx')
- value_grad: float32 [960, 320], P('dp', 'ctx')
- output_grad: float32 [960, 960], P('dp', 'ctx')
- second_gain_grad: float32 [960], P('ctx')
- gate_grad: float32 [960, 2560], P('dp', 'ctx')
- up_grad: float32 [960, 2560], P('dp', 'ctx')
- down_grad: float32 [2560, 960], P('dp', 'ctx')
Inputs may be any that keep to these rules, and one draw needn't show every extreme that they name: `segments`: in each sequence the numbers start at 0 and rise by one at each document boundary; every document holds 60 to 800 tokens except that the last one of a sequence may be cut shorter; one sequence of the whole batch is cut into documents of exactly 60 tokens; every data index holds one other sequence that is a single document, except the data index of that cut sequence where 2 is 1.
All inputs are finite; a program needn't handle non-finite values.
Results may differ from a plain program's by a relative error of at most 0.022.
Values may be sent and summed in bfloat16 or wider, within the bound.
No kernel may reach another device: no remote copies, remote signals or barrier semaphores. Data moves between devices by JAX's collectives and lax.ppermute only.
A program may use at most 256 MiB of HBM per device.

v0:
```python
import math

import jax
import jax.numpy as jnp
from jax import lax
from jax.sharding import PartitionSpec as P

HEAD_SIZE = 64


def rope_tables(first, count_items):
    place = (first + jnp.arange(count_items, dtype=jnp.int32)).astype(jnp.float32)
    freq = jnp.exp(
        -math.log(10000.0)
        * jnp.arange(HEAD_SIZE // 2, dtype=jnp.int32).astype(jnp.float32)
        * 2.0
        / HEAD_SIZE
    )
    angle = place[:, None] * freq[None, :]
    return (jnp.cos(angle), jnp.sin(angle))


def rotate_halves(field, cosine_table, sine_table):
    first = field[..., : HEAD_SIZE // 2]
    second = field[..., HEAD_SIZE // 2 :]
    cosine_table = cosine_table[None, :, None, :]
    sine_table = sine_table[None, :, None, :]
    return jnp.concatenate(
        [first * cosine_table - second * sine_table, second * cosine_table + first * sine_table],
        axis=-1,
    )


def collect(
    query_weight,
    key_matrix,
    value_matrix,
    output_weight,
    gate_weight,
    up_weight,
    down_weight,
    attn_gain,
    second_gain,
):
    parts = (
        lax.all_gather(query_weight, "ctx", axis=1, tiled=True),
        lax.all_gather(key_matrix, "ctx", axis=1, tiled=True),
        lax.all_gather(value_matrix, "ctx", axis=1, tiled=True),
        lax.all_gather(output_weight, "ctx", axis=1, tiled=True),
        lax.all_gather(gate_weight, "ctx", axis=1, tiled=True),
        lax.all_gather(up_weight, "ctx", axis=1, tiled=True),
        lax.all_gather(down_weight, "ctx", axis=1, tiled=True),
        lax.all_gather(attn_gain, "ctx", axis=0, tiled=True),
        lax.all_gather(second_gain, "ctx", axis=0, tiled=True),
    )
    qpart, kpart, vpart, opart, gpart, upart, dpart, first_gain, later_gain = parts
    whole = (
        lax.all_gather(qpart, "dp", axis=0, tiled=True),
        lax.all_gather(kpart, "dp", axis=0, tiled=True),
        lax.all_gather(vpart, "dp", axis=0, tiled=True),
        lax.all_gather(opart, "dp", axis=0, tiled=True),
        lax.all_gather(gpart, "dp", axis=0, tiled=True),
        lax.all_gather(upart, "dp", axis=0, tiled=True),
        lax.all_gather(dpart, "dp", axis=0, tiled=True),
    )
    return tuple(whole) + (first_gain, later_gain)


def norm_back(dnorm, value, scale, gain):
    dgain = jnp.sum(dnorm * value * scale, axis=(0, 1))
    scaled = dnorm * gain
    dvalue = scale * (
        scaled - value * scale * scale * jnp.mean(scaled * value, axis=-1, keepdims=True)
    )
    return (dvalue, dgain)


def split_blocks(key_rows, value_rows, segs):
    seqs, count_all, features = key_rows.shape
    size = math.gcd(count_all, 256)
    count_items = count_all // size
    heads_kv = features // HEAD_SIZE
    key_blocks = jnp.moveaxis(key_rows.reshape(seqs, count_items, size, heads_kv, HEAD_SIZE), 1, 0)
    value_blocks = jnp.moveaxis(
        value_rows.reshape(seqs, count_items, size, heads_kv, HEAD_SIZE), 1, 0
    )
    seg_blocks = jnp.moveaxis(segs.reshape(seqs, count_items, size), 1, 0)
    return (key_blocks, value_blocks, seg_blocks, size, count_items)


def body(
    tokens,
    segments,
    cotangent,
    attn_gain,
    query_weight,
    key_matrix,
    value_matrix,
    output_weight,
    second_gain,
    gate_weight,
    up_weight,
    down_weight,
):
    shards = (
        query_weight,
        key_matrix,
        value_matrix,
        output_weight,
        gate_weight,
        up_weight,
        down_weight,
        attn_gain,
        second_gain,
    )
    q_full, k_full, v_full, o_full, g_full, u_full, d_full, first_gain, later_gain = collect(
        *shards
    )
    seqs, span, width = tokens.shape
    heads_kv = k_full.shape[1] // HEAD_SIZE
    heads_q = q_full.shape[1] // HEAD_SIZE
    head_ratio = heads_q // heads_kv
    scale = HEAD_SIZE ** (-0.5)
    first = lax.axis_index("ctx") * span
    last_place = first + span - 1
    cosine_table, sine_table = rope_tables(first, span)
    qplace = first + jnp.arange(span, dtype=jnp.int32)
    inputs = tokens.astype(jnp.float32)
    gain_one = first_gain.astype(jnp.float32)
    gain_two = later_gain.astype(jnp.float32)
    scale_one = lax.rsqrt(jnp.mean(inputs * inputs, axis=-1, keepdims=True) + 1e-05)
    first_hidden = (inputs * scale_one * gain_one).astype(jnp.bfloat16)
    query_rows = jnp.einsum("scd,df->scf", first_hidden, q_full, preferred_element_type=jnp.float32)
    query_rot = rotate_halves(
        query_rows.reshape(seqs, span, heads_q, HEAD_SIZE), cosine_table, sine_table
    ).astype(jnp.bfloat16)
    keyed = jnp.einsum("scd,df->scf", first_hidden, k_full, preferred_element_type=jnp.float32)
    key_rot = (
        rotate_halves(keyed.reshape(seqs, span, heads_kv, HEAD_SIZE), cosine_table, sine_table)
        .astype(jnp.bfloat16)
        .reshape(seqs, span, heads_kv * HEAD_SIZE)
    )
    valued = jnp.einsum(
        "scd,df->scf", first_hidden, v_full, preferred_element_type=jnp.float32
    ).astype(jnp.bfloat16)
    query_heads = query_rot.reshape(seqs, span, heads_kv, head_ratio, HEAD_SIZE).transpose(
        0, 2, 3, 1, 4
    )

    def masked_scores(key_block, seg_block, kplace):
        raw = jnp.einsum(
            "shgcd,snhd->shgcn", query_heads, key_block, preferred_element_type=jnp.float32
        )
        allowed = (kplace[None, None, :] <= qplace[None, :, None]) & (
            segments[:, :, None] == seg_block[:, None, :]
        )
        return jnp.where(allowed[:, None, None], raw * scale, -jnp.inf)

    init = (
        jnp.full((seqs, heads_kv, head_ratio, span), -1e30, jnp.float32),
        jnp.zeros((seqs, heads_kv, head_ratio, span), jnp.float32),
        jnp.zeros((seqs, heads_kv, head_ratio, span, HEAD_SIZE), jnp.float32),
    )
    carry = init
    key_blocks, value_blocks, seg_blocks, fold_size, count_items = split_blocks(
        lax.all_gather(key_rot, "ctx", axis=1, tiled=True),
        lax.all_gather(valued, "ctx", axis=1, tiled=True),
        lax.all_gather(segments, "ctx", axis=1, tiled=True),
    )
    offsets = jnp.arange(count_items, dtype=jnp.int32) * fold_size

    def one_block(state, item):
        key_block, value_block, seg_block, offset = item

        def one_compute(current):
            top, total, accum = current
            scores = masked_scores(
                key_block, seg_block, offset + jnp.arange(fold_size, dtype=jnp.int32)
            )
            new_top = jnp.maximum(top, jnp.max(scores, axis=-1))
            shrink = jnp.exp(top - new_top)
            weight = jnp.exp(scores - new_top[..., None])
            total = total * shrink + jnp.sum(weight, axis=-1)
            accum = accum * shrink[..., None] + jnp.einsum(
                "shgcn,snhd->shgcd",
                weight.astype(jnp.bfloat16),
                value_block,
                preferred_element_type=jnp.float32,
            )
            return (new_top, total, accum)

        def unchanged(current):
            return current

        return (lax.cond(offset <= last_place, one_compute, unchanged, state), None)

    carry, unused = lax.scan(one_block, carry, (key_blocks, value_blocks, seg_blocks, offsets))
    top, total, accum = carry
    log_total = top + jnp.log(total)
    attended = accum / total[..., None]
    attended_out = (
        attended.transpose(0, 3, 1, 2, 4)
        .reshape(seqs, span, heads_q * HEAD_SIZE)
        .astype(jnp.bfloat16)
    )
    after_attn = inputs + jnp.einsum(
        "scf,fd->scd", attended_out, o_full, preferred_element_type=jnp.float32
    )
    scale_two = lax.rsqrt(jnp.mean(after_attn * after_attn, axis=-1, keepdims=True) + 1e-05)
    hidden_two = (after_attn * scale_two * gain_two).astype(jnp.bfloat16)
    gate = jnp.einsum("scd,df->scf", hidden_two, g_full, preferred_element_type=jnp.float32)
    upward = jnp.einsum("scd,df->scf", hidden_two, u_full, preferred_element_type=jnp.float32)
    sigma = jax.nn.sigmoid(gate)
    active = gate * sigma
    inner = (active * upward).astype(jnp.bfloat16)
    result = after_attn + jnp.einsum(
        "scf,fd->scd", inner, d_full, preferred_element_type=jnp.float32
    )
    block_output = result.astype(jnp.bfloat16)
    q_full, k_full, v_full, o_full, g_full, u_full, d_full, first_gain, later_gain = collect(
        *shards
    )
    gain_one = first_gain.astype(jnp.float32)
    gain_two = later_gain.astype(jnp.float32)
    grad_low = cotangent.astype(jnp.bfloat16)
    down_term = jnp.einsum("scf,scd->fd", inner, grad_low, preferred_element_type=jnp.float32)
    dinner = jnp.einsum("scd,fd->scf", grad_low, d_full, preferred_element_type=jnp.float32)
    dgate = (dinner * upward * sigma * (1.0 + gate * (1.0 - sigma))).astype(jnp.bfloat16)
    dupward = (dinner * active).astype(jnp.bfloat16)
    gate_term = jnp.einsum("scd,scf->df", hidden_two, dgate, preferred_element_type=jnp.float32)
    up_term = jnp.einsum("scd,scf->df", hidden_two, dupward, preferred_element_type=jnp.float32)
    dhidden_two = jnp.einsum(
        "scf,df->scd", dgate, g_full, preferred_element_type=jnp.float32
    ) + jnp.einsum("scf,df->scd", dupward, u_full, preferred_element_type=jnp.float32)
    dnorm_two, second_term = norm_back(dhidden_two, after_attn, scale_two, gain_two)
    dafter = cotangent + dnorm_two
    dattn_low = dafter.astype(jnp.bfloat16)
    output_term = jnp.einsum(
        "scf,scd->fd", attended_out, dattn_low, preferred_element_type=jnp.float32
    )
    dattended = jnp.einsum(
        "scd,fd->scf", dattn_low, o_full, preferred_element_type=jnp.float32
    ).astype(jnp.bfloat16)
    dout_heads = dattended.reshape(seqs, span, heads_kv, head_ratio, HEAD_SIZE).transpose(
        0, 2, 3, 1, 4
    )
    delta = jnp.sum(dout_heads.astype(jnp.float32) * attended, axis=-1)
    keys_all, values_all, segs_all = (
        lax.all_gather(key_rot, "ctx", axis=1, tiled=True),
        lax.all_gather(valued, "ctx", axis=1, tiled=True),
        lax.all_gather(segments, "ctx", axis=1, tiled=True),
    )
    key_blocks, value_blocks, seg_blocks, size, count_items = split_blocks(
        keys_all, values_all, segs_all
    )
    offsets = jnp.arange(count_items, dtype=jnp.int32) * size

    def back_block(dquery, item):
        key_block, value_block, seg_block, offset = item

        def back_compute(current):
            scores = masked_scores(key_block, seg_block, offset + jnp.arange(size, dtype=jnp.int32))
            prob = jnp.exp(scores - log_total[..., None])
            prob_low = prob.astype(jnp.bfloat16)
            dvalue = jnp.einsum(
                "shgcn,shgcd->snhd", prob_low, dout_heads, preferred_element_type=jnp.float32
            )
            dprob = jnp.einsum(
                "shgcd,snhd->shgcn", dout_heads, value_block, preferred_element_type=jnp.float32
            )
            dscore = (prob * (dprob - delta[..., None]) * scale).astype(jnp.bfloat16)
            current = current + jnp.einsum(
                "shgcn,snhd->shgcd", dscore, key_block, preferred_element_type=jnp.float32
            )
            dkey = jnp.einsum(
                "shgcn,shgcd->snhd", dscore, query_heads, preferred_element_type=jnp.float32
            )
            return (current, dkey, dvalue)

        def skipped(current):
            empty = jnp.zeros((seqs, size, heads_kv, HEAD_SIZE), jnp.float32)
            return (current, empty, empty)

        dquery, dkey, dvalue = lax.cond(offset <= last_place, back_compute, skipped, dquery)
        return (dquery, (dkey, dvalue))

    dquery, (dkey_blocks, dvalue_blocks) = lax.scan(
        back_block,
        jnp.zeros((seqs, heads_kv, head_ratio, span, HEAD_SIZE), jnp.float32),
        (key_blocks, value_blocks, seg_blocks, offsets),
    )
    length_tokens = keys_all.shape[1]
    dkey_all = jnp.moveaxis(dkey_blocks, 0, 1).reshape(seqs, length_tokens, heads_kv * HEAD_SIZE)
    dvalue_all = jnp.moveaxis(dvalue_blocks, 0, 1).reshape(
        seqs, length_tokens, heads_kv * HEAD_SIZE
    )
    dkey_own, dvalue_own = (
        lax.psum_scatter(
            dkey_all.astype(jnp.bfloat16), "ctx", scatter_dimension=1, tiled=True
        ).astype(jnp.float32),
        lax.psum_scatter(
            dvalue_all.astype(jnp.bfloat16), "ctx", scatter_dimension=1, tiled=True
        ).astype(jnp.float32),
    )
    dquery_flat = dquery.transpose(0, 3, 1, 2, 4).reshape(seqs, span, heads_q, HEAD_SIZE)
    dquery_low = (
        rotate_halves(dquery_flat, cosine_table, -sine_table)
        .astype(jnp.bfloat16)
        .reshape(seqs, span, heads_q * HEAD_SIZE)
    )
    dkey_low = (
        rotate_halves(dkey_own.reshape(seqs, span, heads_kv, HEAD_SIZE), cosine_table, -sine_table)
        .astype(jnp.bfloat16)
        .reshape(seqs, span, heads_kv * HEAD_SIZE)
    )
    dvalue_low = dvalue_own.astype(jnp.bfloat16)
    query_term = jnp.einsum(
        "scd,scf->df", first_hidden, dquery_low, preferred_element_type=jnp.float32
    )
    key_term = jnp.einsum("scd,scf->df", first_hidden, dkey_low, preferred_element_type=jnp.float32)
    value_term = jnp.einsum(
        "scd,scf->df", first_hidden, dvalue_low, preferred_element_type=jnp.float32
    )
    dhidden_one = jnp.einsum("scf,df->scd", dquery_low, q_full, preferred_element_type=jnp.float32)
    dhidden_one = dhidden_one + jnp.einsum(
        "scf,df->scd", dkey_low, k_full, preferred_element_type=jnp.float32
    )
    dhidden_one = dhidden_one + jnp.einsum(
        "scf,df->scd", dvalue_low, v_full, preferred_element_type=jnp.float32
    )
    dnorm_one, first_term = norm_back(dhidden_one, inputs, scale_one, gain_one)
    input_grad = dafter + dnorm_one
    summed = (
        lax.psum_scatter(
            query_term.astype(jnp.bfloat16), "dp", scatter_dimension=0, tiled=True
        ).astype(jnp.float32),
        lax.psum_scatter(
            key_term.astype(jnp.bfloat16), "dp", scatter_dimension=0, tiled=True
        ).astype(jnp.float32),
        lax.psum_scatter(
            value_term.astype(jnp.bfloat16), "dp", scatter_dimension=0, tiled=True
        ).astype(jnp.float32),
        lax.psum_scatter(
            output_term.astype(jnp.bfloat16), "dp", scatter_dimension=0, tiled=True
        ).astype(jnp.float32),
        lax.psum_scatter(
            gate_term.astype(jnp.bfloat16), "dp", scatter_dimension=0, tiled=True
        ).astype(jnp.float32),
        lax.psum_scatter(
            up_term.astype(jnp.bfloat16), "dp", scatter_dimension=0, tiled=True
        ).astype(jnp.float32),
        lax.psum_scatter(
            down_term.astype(jnp.bfloat16), "dp", scatter_dimension=0, tiled=True
        ).astype(jnp.float32),
    )
    q_sum, k_sum, v_sum, o_sum, g_sum, u_sum, d_sum = summed
    owned = (
        lax.psum_scatter(q_sum.astype(jnp.bfloat16), "ctx", scatter_dimension=1, tiled=True).astype(
            jnp.float32
        ),
        lax.psum_scatter(k_sum.astype(jnp.bfloat16), "ctx", scatter_dimension=1, tiled=True).astype(
            jnp.float32
        ),
        lax.psum_scatter(v_sum.astype(jnp.bfloat16), "ctx", scatter_dimension=1, tiled=True).astype(
            jnp.float32
        ),
        lax.psum_scatter(o_sum.astype(jnp.bfloat16), "ctx", scatter_dimension=1, tiled=True).astype(
            jnp.float32
        ),
        lax.psum_scatter(g_sum.astype(jnp.bfloat16), "ctx", scatter_dimension=1, tiled=True).astype(
            jnp.float32
        ),
        lax.psum_scatter(u_sum.astype(jnp.bfloat16), "ctx", scatter_dimension=1, tiled=True).astype(
            jnp.float32
        ),
        lax.psum_scatter(d_sum.astype(jnp.bfloat16), "ctx", scatter_dimension=1, tiled=True).astype(
            jnp.float32
        ),
        lax.psum_scatter(
            first_term.astype(jnp.bfloat16), "ctx", scatter_dimension=0, tiled=True
        ).astype(jnp.float32),
        lax.psum_scatter(
            second_term.astype(jnp.bfloat16), "ctx", scatter_dimension=0, tiled=True
        ).astype(jnp.float32),
    )
    q_grad, k_grad, v_grad, o_grad, g_grad, u_grad, d_grad, first_part, second_part = owned
    first_grad, second_grad = lax.psum((first_part, second_part), "dp")
    return (
        block_output,
        input_grad,
        first_grad,
        q_grad,
        k_grad,
        v_grad,
        o_grad,
        second_grad,
        g_grad,
        u_grad,
        d_grad,
    )


def solution(mesh):
    placed = (
        P("dp", "ctx", None),
        P("dp", "ctx"),
        P("dp", "ctx", None),
        P("ctx"),
        P("dp", "ctx"),
        P("dp", "ctx"),
        P("dp", "ctx"),
        P("dp", "ctx"),
        P("ctx"),
        P("dp", "ctx"),
        P("dp", "ctx"),
        P("dp", "ctx"),
    )
    return jax.shard_map(
        body,
        mesh=mesh,
        in_specs=placed,
        out_specs=(
            P("dp", "ctx", None),
            P("dp", "ctx", None),
            P("ctx"),
            P("dp", "ctx"),
            P("dp", "ctx"),
            P("dp", "ctx"),
            P("dp", "ctx"),
            P("ctx"),
            P("dp", "ctx"),
            P("dp", "ctx"),
            P("dp", "ctx"),
        ),
        check_vma=False,
    )
```

profile of v0, /device:TPU:0, one launch (start us, length us, event | category | flops | bytes accessed | tf_op | source)
XLA Modules:
  0.0 1609.4 jit_solution(8179492149932576090)
XLA Ops:
  21.9 33.1 %all-gather = bf16[8,120,320]{1,2,0:T(8,128)(2,1)S(1)} all-gather(bf16[1,120,320]{1,2,0:T(8,128)(2,1)S(1)} %bitcast.280), channel_id=1, replica_groups=mesh['dp'=8,'ctx'=4] {'dp'}, dimensions={0}, use_global_device_ids=true | all-gather | bytes 691200 | tf_op jit(solution)/shard_map/all_gather | solution.py:59
  72.8 31.8 %all-gather.1 = bf16[8,120,320]{1,2,0:T(8,128)(2,1)S(1)} all-gather(bf16[1,120,320]{1,2,0:T(8,128)(2,1)S(1)} %bitcast.281), channel_id=1, replica_groups=mesh['dp'=8,'ctx'=4] {'dp'}, dimensions={0}, use_global_device_ids=true | all-gather | bytes 691200 | tf_op jit(solution)/shard_map/all_gather | solution.py:60
  172.4 73.1 %while.33 = (s32[]{:T(128)}, f32[2,5,3,512]{3,2,1,0:T(4,128)S(1)}, f32[2,5,3,512]{3,2,1,0:T(4,128)S(1)}, f32[2,5,3,512,64]{3,4,2,1,0:T(8,128)}, s32[8]{0:T(128)S...) while((s32[]{:T(128)}, f32[2,5,3,512]{3,2,1,0:T(4,128)S(1)}, ...), condition=%wide.region_6.7_spmd.clone, body=%wide.region_1.6_spmd.clone.sunk | while | flops 1052539648 | bytes 59987264 | solution.py:197
  173.8 31.0 %conditional.6 = ((f32[2,5,3,512]{3,2,1,0:T(4,128)S(1)}, f32[2,5,3,512]{3,2,1,0:T(4,128)S(1)}, f32[2,5,3,512,64]{3,4,2,1,0:T(8,128)})) conditional(s32[]{:T(128)} %convert_element_type.323, (f32[2,5,3,512]{3,2,1,0:T(4,128)S(1)}, f32[2,5,3,512]{3,2,1,0:T(4,128)S(1)}, f32[2,5,3,512,64]{3,4,2,1,0:T(8,128)}) %tuple.98, (s32[]{:T(128)}, s32[]{:T(128)}, ...), branch_computations={%region_2.2_spmd, %region_3.5_spmd} | conditional | flops 1052539648 | bytes 59984940 | solution.py:195
  206.0 31.6 %conditional.6 = ((f32[2,5,3,512]{3,2,1,0:T(4,128)S(1)}, f32[2,5,3,512]{3,2,1,0:T(4,128)S(1)}, f32[2,5,3,512,64]{3,4,2,1,0:T(8,128)})) conditional(s32[]{:T(128)} %convert_element_type.323, (f32[2,5,3,512]{3,2,1,0:T(4,128)S(1)}, f32[2,5,3,512]{3,2,1,0:T(4,128)S(1)}, f32[2,5,3,512,64]{3,4,2,1,0:T(8,128)}) %tuple.98, (s32[]{:T(128)}, s32[]{:T(128)}, ...), branch_computations={%region_2.2_spmd, %region_3.5_spmd} | conditional | flops 1052539648 | bytes 59984940 | solution.py:195
  285.1 75.9 %all-gather.23.cloned.1.call-done = bf16[2560,960]{1,0:T(8,128)(2,1)} async-done(((bf16[320,960]{1,0:T(8,128)(2,1)}), bf16[2560,960]{1,0:T(8,128)(2,1)}) %all-gather.23.cloned.1.call-update) | async-done | bytes 4915216 | tf_op jit(solution)/shard_map/all_gather | solution.py:64
  372.2 71.4 %all-gather.19.cloned.1.call-done = bf16[960,2560]{1,0:T(8,128)(2,1)} async-done(((bf16[120,2560]{1,0:T(8,128)(2,1)}), bf16[960,2560]{1,0:T(8,128)(2,1)}) %all-gather.19.cloned.1.call-update) | async-done | bytes 4915216 | tf_op jit(solution)/shard_map/all_gather | solution.py:62
  443.6 20.4 %multiply_convert_fusion.1 = (bf16[2,512,2560]{2,1,0:T(8,128)(2,1)}, bf16[2,512,2560]{2,1,0:T(8,128)(2,1)}, bf16[2,512,2560]{2,1,0:T(8,128)(2,1)}) fusion(f32[2,512,2560]{2,1,0:T(8,128)} %fusion.45, f32[2,512,2560]{2,1,0:T(8,128)} %fusion.51, bf16[2,512,960]{1,2,0:T(8,128)(2,1)} %multiply_convert_fusion.3, bf16[960,2560]{1,0:T(8,128)(2,1)} %all-gather.19.cloned.1.call-done), kind=kOutput, calls=%fused_computation.59 | convolution fusion | flops 5072486400 | bytes 43581440 | tf_op jit(solution)/shard_map/scd,df->scf/dot_general | solution.py:211
  489.1 90.6 %while.34 = (s32[]{:T(128)}, f32[2,5,3,512,64]{3,4,2,1,0:T(8,128)}, bf16[8,2,256,5,64]{2,4,3,1,0:T(8,128)(2,1)}, bf16[8,2,256,5,64]{2,4,3,1,0:T(8,128)(2,1)}, s3...) while((s32[]{:T(128)}, f32[2,5,3,512,64]{3,4,2,1,0:T(8,128)}, ...), condition=%wide.region_13.14_spmd.clone, body=%wide.region_10.13_spmd.clone.sunk | while | flops 2561475328 | bytes 98576736 | solution.py:287
  490.5 36.1 %conditional.7 = (f32[2,5,3,512,64]{3,4,2,1,0:T(8,128)}, bf16[1,2,256,5,64]{2,4,3,1,0:T(8,128)(2,1)S(1)}, bf16[1,2,256,5,64]{2,4,3,1,0:T(8,128)(2,1)S(1)}) conditional(s32[]{:T(128)} %convert_element_type.324, f32[2,5,3,512,64]{3,4,2,1,0:T(8,128)} %get-tuple-element.865, (s32[]{:T(128)}, s32[]{:T(128)}, s32[2,512]{1,0:T(2,128)S(1)}, ...), branch_computations={%region_11.11_spmd, %region_12.12_spmd} | conditional | flops 2561475328 | bytes 97263168 | solution.py:284
  528.8 36.1 %conditional.7 = (f32[2,5,3,512,64]{3,4,2,1,0:T(8,128)}, bf16[1,2,256,5,64]{2,4,3,1,0:T(8,128)(2,1)S(1)}, bf16[1,2,256,5,64]{2,4,3,1,0:T(8,128)(2,1)S(1)}) conditional(s32[]{:T(128)} %convert_element_type.324, f32[2,5,3,512,64]{3,4,2,1,0:T(8,128)} %get-tuple-element.865, (s32[]{:T(128)}, s32[]{:T(128)}, s32[2,512]{1,0:T(2,128)S(1)}, ...), branch_computations={%region_11.11_spmd, %region_12.12_spmd} | conditional | flops 2561475328 | bytes 97263168 | solution.py:284
  607.4 252.9 %reduce-scatter.27.cloned.1.call-done = bf16[2,512,320]{1,2,0:T(8,128)(2,1)} async-done(((bf16[2,2048,320]{1,2,0:T(8,128)(2,1)}), bf16[2,512,320]{1,2,0:T(8,128)(2,1)}) %reduce-scatter.27.cloned.1.call-update) | async-done | bytes 655376 | tf_op jit(solution)/shard_map/reduce_scatter | solution.py:298
  863.6 34.1 %reduce-scatter.29.cloned.1.call-done = bf16[2,512,320]{1,2,0:T(8,128)(2,1)} async-done(((bf16[2,2048,320]{1,2,0:T(8,128)(2,1)}), bf16[2,512,320]{1,2,0:T(8,128)(2,1)}) %reduce-scatter.29.cloned.1.call-update) | async-done | bytes 655376 | tf_op jit(solution)/shard_map/reduce_scatter | solution.py:301
  920.4 47.3 %reduce-scatter.31.cloned.1.call-done = bf16[120,960]{1,0:T(8,128)(2,1)} async-done(((bf16[960,960]{1,0:T(8,128)(2,1)}), bf16[120,960]{1,0:T(8,128)(2,1)}) %reduce-scatter.31.cloned.1.call-update) | async-done | bytes 230416 | tf_op jit(solution)/shard_map/reduce_scatter | solution.py:334
  969.6 67.8 %reduce-scatter.37.cloned.1.call-done = bf16[120,960]{1,0:T(8,128)(2,1)} async-done(((bf16[960,960]{1,0:T(8,128)(2,1)}), bf16[120,960]{1,0:T(8,128)(2,1)}) %reduce-scatter.37.cloned.1.call-update) | async-done | bytes 230416 | tf_op jit(solution)/shard_map/reduce_scatter | solution.py:343
  1051.5 72.7 %all-reduce.12.cloned.1.call-done = (bf16[960,320]{0,1:T(8,128)(2,1)}, bf16[960,320]{0,1:T(8,128)(2,1)}) async-done(((bf16[960,320]{0,1:T(8,128)(2,1)}, bf16[960,320]{0,1:T(8,128)(2,1)}), (bf16[960,320]{0,1:T(8,128)(2,1)}, bf16[960,320]{0,1:T(8,128)(2,1)})) %all-reduce.12.cloned.1.call-update) | async-done | bytes 1228816
  1127.7 98.5 %reduce-scatter.39.cloned.1.call-done = bf16[120,2560]{1,0:T(8,128)(2,1)} async-done(((bf16[960,2560]{1,0:T(8,128)(2,1)}), bf16[120,2560]{1,0:T(8,128)(2,1)}) %reduce-scatter.39.cloned.1.call-update) | async-done | bytes 614416 | tf_op jit(solution)/shard_map/reduce_scatter | solution.py:346
  1229.1 99.1 %reduce-scatter.41.cloned.1.call-done = bf16[120,2560]{1,0:T(8,128)(2,1)} async-done(((bf16[960,2560]{1,0:T(8,128)(2,1)}), bf16[120,2560]{1,0:T(8,128)(2,1)}) %reduce-scatter.41.cloned.1.call-update) | async-done | bytes 614416 | tf_op jit(solution)/shard_map/reduce_scatter | solution.py:349
  1352.6 21.3 %reduce-scatter.47.cloned.1.call-done = bf16[240,120]{1,0:T(8,128)(2,1)} async-done(((bf16[960,120]{1,0:T(8,128)(2,1)}), bf16[240,120]{1,0:T(8,128)(2,1)}) %reduce-scatter.47.cloned.1.call-update) | async-done | bytes 57616
  1378.6 101.7 %reduce-scatter.43.cloned.1.call-done = bf16[320,960]{1,0:T(8,128)(2,1)} async-done(((bf16[2560,960]{1,0:T(8,128)(2,1)}), bf16[320,960]{1,0:T(8,128)(2,1)}) %reduce-scatter.43.cloned.1.call-update) | async-done | bytes 614416 | tf_op jit(solution)/shard_map/reduce_scatter | solution.py:352
  1496.7 21.2 %all-reduce.6 = (f32[240]{0:T(256)}, f32[240]{0:T(256)}) all-reduce(f32[240]{0:T(256)S(1)} %get-tuple-element.616, f32[240]{0:T(256)S(1)} %get-tuple-element.615), channel_id=1, replica_groups=mesh['dp'=8,'ctx'=4] {'dp'}, use_global_device_ids=true, to_apply=%region_19.20 | all-reduce | flops 480 | bytes 3840 | tf_op jit(solution)/shard_map/psum | solution.py:387
  1526.9 22.8 %reduce-scatter.49.cloned.1.call-done = bf16[640,120]{1,0:T(8,128)(2,1)} async-done(((bf16[2560,120]{1,0:T(8,128)(2,1)}), bf16[640,120]{1,0:T(8,128)(2,1)}) %reduce-scatter.49.cloned.1.call-update) | async-done | bytes 153616
  1551.5 23.4 %reduce-scatter.51.cloned.1.call-done = bf16[640,120]{1,0:T(8,128)(2,1)} async-done(((bf16[2560,120]{1,0:T(8,128)(2,1)}), bf16[640,120]{1,0:T(8,128)(2,1)}) %reduce-scatter.51.cloned.1.call-update) | async-done | bytes 153616
  1576.7 23.9 %reduce-scatter.53.cloned.1.call-done = bf16[240,320]{1,0:T(8,128)(2,1)} async-done(((bf16[960,320]{1,0:T(8,128)(2,1)}), bf16[240,320]{1,0:T(8,128)(2,1)}) %reduce-scatter.53.cloned.1.call-update) | async-done | bytes 153616
  (336 shorter events, 461.3 us)
Async XLA Ops:
  7.2 148.4 %all-gather.13.cloned.1.call-start = ((), (), s32[]{:S(2)}) async-start(), calls=%async_computation.15 | async-start | bytes 2211840 | tf_op jit(solution)/shard_map/all_gather | solution.py:58
  16.3 144.1 %all-gather.11.cloned.1.call-start = ((), (), s32[]{:S(2)}) async-start(), calls=%async_computation.14 | async-start | bytes 3276800 | tf_op jit(solution)/shard_map/all_gather | solution.py:166
  63.9 91.7 %copy-start.20 = (f32[960]{0:T(1024)}, f32[960]{0:T(1024)S(1)}, u32[]{:S(2)}) copy-start(f32[960]{0:T(1024)S(1)} %convert_element_type.195) | copy-start | bytes 11524
  65.3 94.3 %copy-start.14 = (f32[512,32]{0,1:T(8,128)}, f32[512,32]{0,1:T(8,128)S(1)}, u32[]{:S(2)}) copy-start(f32[512,32]{0,1:T(8,128)S(1)} %get-tuple-element.608) | copy-start | bytes 196612
  67.4 97.8 %all-gather.15.cloned.1.call-start = ((), (), s32[]{:S(2)}) async-start(), calls=%async_computation.16 | async-start | bytes 3276800 | tf_op jit(solution)/shard_map/all_gather | solution.py:167
  107.4 142.1 %all-gather.17.cloned.1.call-start = ((), (), s32[]{:S(2)}) async-start(), calls=%async_computation.17 | async-start | bytes 2211840 | tf_op jit(solution)/shard_map/all_gather | solution.py:61
  114.3 160.1 %all-gather.21.cloned.1.call-start = ((), (), s32[]{:S(2)}) async-start(), calls=%async_computation.19 | async-start | bytes 5529600 | tf_op jit(solution)/shard_map/all_gather | solution.py:63
  125.9 235.1 %all-gather.23.cloned.1.call-start = ((), (), s32[]{:S(2)}) async-start(), calls=%async_computation.20 | async-start | bytes 5898240 | tf_op jit(solution)/shard_map/all_gather | solution.py:64
  139.8 303.8 %all-gather.19.cloned.1.call-start = ((), (), s32[]{:S(2)}) async-start(), calls=%async_computation.18 | async-start | bytes 5529600 | tf_op jit(solution)/shard_map/all_gather | solution.py:62
  149.8 710.5 %reduce-scatter.27.cloned.1.call-start = ((), (), s32[]{:S(2)}) async-start(), calls=%async_computation.21 | async-start | bytes 3276800 | tf_op jit(solution)/shard_map/reduce_scatter | solution.py:298
  586.4 311.4 %reduce-scatter.29.cloned.1.call-start = ((), (), s32[]{:S(2)}) async-start(), calls=%async_computation.22 | async-start | bytes 3276800 | tf_op jit(solution)/shard_map/reduce_scatter | solution.py:301
  593.0 374.7 %reduce-scatter.31.cloned.1.call-start = ((), (), s32[]{:S(2)}) async-start(), calls=%async_computation.23 | async-start | bytes 2211840 | tf_op jit(solution)/shard_map/reduce_scatter | solution.py:334
  601.0 436.4 %reduce-scatter.37.cloned.1.call-start = ((), (), s32[]{:S(2)}) async-start(), calls=%async_computation.26 | async-start | bytes 2211840 | tf_op jit(solution)/shard_map/reduce_scatter | solution.py:343
  607.4 516.9 %all-reduce.12.cloned.1.call-start = ((), (), s32[]{:S(2)}) async-start(), calls=%async_computation.35 | async-start | bytes 2621440
  900.6 325.6 %reduce-scatter.39.cloned.1.call-start = ((), (), s32[]{:S(2)}) async-start(), calls=%async_computation.27 | async-start | bytes 5529600 | tf_op jit(solution)/shard_map/reduce_scatter | solution.py:346
  910.4 417.8 %reduce-scatter.41.cloned.1.call-start = ((), (), s32[]{:S(2)}) async-start(), calls=%async_computation.28 | async-start | bytes 5529600 | tf_op jit(solution)/shard_map/reduce_scatter | solution.py:349
  920.4 430.6 %reduce-scatter.45.cloned.1.call-start = ((), (), s32[]{:S(2)}) async-start(), calls=%async_computation.30 | async-start | bytes 307200
  969.5 404.3 %reduce-scatter.47.cloned.1.call-start = ((), (), s32[]{:S(2)}) async-start(), calls=%async_computation.31 | async-start | bytes 307200
  1039.2 441.1 %reduce-scatter.43.cloned.1.call-start = ((), (), s32[]{:S(2)}) async-start(), calls=%async_computation.29 | async-start | bytes 5898240 | tf_op jit(solution)/shard_map/reduce_scatter | solution.py:352
  1049.6 474.6 %reduce-scatter.33.cloned.1.call-start = ((), (), s32[]{:S(2)}) async-start(), calls=%async_computation.24 | async-start | bytes 102400 | tf_op jit(solution)/shard_map/reduce_scatter | solution.py:361
  1125.9 399.7 %reduce-scatter.35.cloned.1.call-start = ((), (), s32[]{:S(2)}) async-start(), calls=%async_computation.25 | async-start | bytes 102400 | tf_op jit(solution)/shard_map/reduce_scatter | solution.py:364
  1127.6 422.1 %reduce-scatter.49.cloned.1.call-start = ((), (), s32[]{:S(2)}) async-start(), calls=%async_computation.32 | async-start | bytes 819200
  1228.4 346.5 %reduce-scatter.51.cloned.1.call-start = ((), (), s32[]{:S(2)}) async-start(), calls=%async_computation.33 | async-start | bytes 819200
  1330.4 270.2 %reduce-scatter.53.cloned.1.call-start = ((), (), s32[]{:S(2)}) async-start(), calls=%async_computation.34 | async-start | bytes 921600
  (34 other events, 558.8 us)
Sparse Core Ops, SparseCore 0:
  16.4 52.3 all-gather.12
  71.0 25.3 all-gather.10
  107.5 32.7 all-gather.14
  143.0 47.9 all-gather.16
  193.0 81.3 all-gather.20
  276.4 84.4 all-gather.22
  363.1 80.4 all-gather.18
  586.5 273.7 reduce-scatter.26
  863.0 34.6 reduce-scatter.28
  901.0 66.6 reduce-scatter.30
  971.6 65.7 reduce-scatter.36
  1041.4 82.7 all-reduce.11
  1128.4 97.8 reduce-scatter.38
  1229.7 98.4 reduce-scatter.40
  1331.2 19.7 reduce-scatter.44
  1353.9 19.9 reduce-scatter.46
  1377.7 102.5 reduce-scatter.42
  1483.3 19.2 reduce-scatter.32
  1505.1 19.4 reduce-scatter.34
  1527.2 22.4 reduce-scatter.48
  1552.4 22.4 reduce-scatter.50
  1577.6 22.9 reduce-scatter.52
where the time goes:
time: 1620 us; the launch traced here: 1610 us
  waiting for transfers between devices  1040 us (64%)
  matrix products  254 us (16%)
  blocking collectives  161 us (10%)
  local copies, waits for them, and re-layouts  77.7 us (5%)
  other arithmetic  50.6 us (3%)
  between operations  17.2 us (1%)
    reduce_scatter x1, waiting for transfers between devices, body(): lax.psum_scatter(dkey_all.astype(jnp.bfloat16), 'ctx', scatter_dimension=...  253 us
    unnamed x28, waiting for transfers between devices  170 us
    reduce_scatter x1, waiting for transfers between devices, body(): lax.psum_scatter(down_term.astype(jnp.bfloat16), 'dp', scatter_dimension=...  102 us
    reduce_scatter x1, waiting for transfers between devices, body(): lax.psum_scatter(up_term.astype(jnp.bfloat16), 'dp', scatter_dimension=0,...  99.1 us
    reduce_scatter x1, waiting for transfers between devices, body(): lax.psum_scatter(gate_term.astype(jnp.bfloat16), 'dp', scatter_dimension=...  98.5 us
    all_gather x1, waiting for transfers between devices, collect(): lax.all_gather(dpart, 'dp', axis=0, tiled=True)  75.9 us
    all_gather x1, waiting for transfers between devices, collect(): lax.all_gather(gpart, 'dp', axis=0, tiled=True)  71.4 us
    reduce_scatter x1, waiting for transfers between devices, body(): lax.psum_scatter(output_term.astype(jnp.bfloat16), 'dp', scatter_dimensio...  67.8 us
  transfers between devices with their start and end apart: 22, of which 16 were waited for; matrix products, arithmetic and copies ran while one was open for 15% of the time, Pallas kernels for 0%

commit v1 on v0

v1 whole, which is shorter than its diff:
```python
import functools
import math

import jax
import jax.numpy as jnp
from jax import lax
from jax.experimental import pallas as pl
from jax.experimental.pallas import tpu as pltpu
from jax.sharding import PartitionSpec as P

HEAD_SIZE = 64
HALF = HEAD_SIZE // 2
LOW = -1e30
F32 = jnp.float32
BF16 = jnp.bfloat16


def rope_tables(first, count_items):
    place = (first + jnp.arange(count_items, dtype=jnp.int32)).astype(F32)
    freq = jnp.exp(-math.log(10000.0) * jnp.arange(HALF, dtype=jnp.int32).astype(F32) * 2.0 / HEAD_SIZE)
    angle = freq[:, None] * place[None, :]
    return (jnp.cos(angle), jnp.sin(angle))


def rotate_rows(field, cosine, sine):
    seqs, features, span = field.shape
    parts = field.reshape(seqs, features // HEAD_SIZE, 2, HALF, span)
    a, b = parts[:, :, 0], parts[:, :, 1]
    return jnp.stack([a * cosine - b * sine, b * cosine + a * sine], axis=2).reshape(field.shape)


def contract(left, right, axes):
    return lax.dot_general(left, right, ((axes[:1], axes[1:]), ((), ())), preferred_element_type=F32)


def side_by_side(ref, heads, tile, size):
    cut = pl.ds(tile * size, size)
    return jnp.concatenate([ref[0, g * HEAD_SIZE : (g + 1) * HEAD_SIZE, cut] for g in range(heads)], axis=1)


def allowed_keys(j, size, start, place):
    key = j * size + lax.broadcasted_iota(jnp.int32, (size, start.shape[1]), 0)
    return (key >= start) & (key <= place)


def attend_kernel(heads, size, bounds, q_ref, kv_ref, rows_ref, o_ref, lse_ref):
    seq = pl.program_id(0)
    tiles = q_ref.shape[2] // size
    for t in range(tiles):
        q = side_by_side(q_ref, heads, t, size) * BF16(HEAD_SIZE**-0.5)
        cut = pl.ds(t * size, size)
        start = jnp.concatenate([rows_ref[0, 0:1, cut]] * heads, axis=1)
        place = jnp.concatenate([rows_ref[0, 1:2, cut]] * heads, axis=1)

        def one(j, state, masked):
            top, total, acc = state
            s = contract(kv_ref[j, 0, 0, 0], q, (0, 0))
            if masked:
                s = jnp.where(allowed_keys(j, size, start, place), s, LOW)
            new = jnp.maximum(top, jnp.max(s, axis=0, keepdims=True))
            shrink = jnp.exp(top - new)
            p = jnp.exp(s - new)
            total = total * shrink + jnp.sum(p, axis=0, keepdims=True)
            acc = acc * shrink + contract(kv_ref[j, 0, 1, 0], p.astype(BF16), (1, 0))
            return (new, total, acc)

        lanes = heads * size
        state = (jnp.full((1, lanes), LOW, F32), jnp.zeros((1, lanes), F32), jnp.zeros((HEAD_SIZE, lanes), F32))
        lo, mid, diag = (bounds[3 * (seq * tiles + t) + k] for k in range(3))
        state = lax.fori_loop(lo, mid, lambda j, c: one(j, c, True), state)
        state = lax.fori_loop(mid, diag, lambda j, c: one(j, c, False), state)
        top, total, acc = one(diag, state, True)
        out = (acc / total).astype(BF16)
        lse = top + jnp.log(total)
        for g in range(heads):
            o_ref[0, g * HEAD_SIZE : (g + 1) * HEAD_SIZE, cut] = out[:, g * size : (g + 1) * size]
            lse_ref[0, 0, g : g + 1, cut] = lse[:, g * size : (g + 1) * size]


def back_kernel(heads, size, bounds, q_ref, kv_ref, rows_ref, o_ref, do_ref, lse_ref, cos_ref, sin_ref, dq_ref, dkv_ref, sums):
    seq = pl.program_id(0)
    tiles = q_ref.shape[2] // size
    sums[...] = jnp.zeros_like(sums)
    for t in range(tiles):
        q = side_by_side(q_ref, heads, t, size) * BF16(HEAD_SIZE**-0.5)
        do = side_by_side(do_ref, heads, t, size)
        o = side_by_side(o_ref, heads, t, size)
        delta = jnp.sum(do.astype(F32) * o.astype(F32), axis=0, keepdims=True)
        cut = pl.ds(t * size, size)
        start = jnp.concatenate([rows_ref[0, 0:1, cut]] * heads, axis=1)
        place = jnp.concatenate([rows_ref[0, 1:2, cut]] * heads, axis=1)
        lse = jnp.concatenate([lse_ref[0, 0, g : g + 1, cut] for g in range(heads)], axis=1)

        def one(j, dq, masked):
            k, v = kv_ref[j, 0, 0, 0], kv_ref[j, 0, 1, 0]
            p = jnp.exp(contract(k, q, (0, 0)) - lse)
            if masked:
                p = jnp.where(allowed_keys(j, size, start, place), p, 0.0)
            dp = contract(v, do, (0, 0))
            ds = (p * (dp - delta)).astype(BF16)
            sums[j, 0] += contract(q, ds, (1, 1))
            sums[j, 1] += contract(do, p.astype(BF16), (1, 1))
            return dq + contract(k, ds, (1, 0))

        dq = jnp.zeros((HEAD_SIZE, heads * size), F32)
        lo, mid, diag = (bounds[3 * (seq * tiles + t) + k] for k in range(3))
        dq = lax.fori_loop(lo, mid, lambda j, c: one(j, c, True), dq)
        dq = lax.fori_loop(mid, diag, lambda j, c: one(j, c, False), dq)
        dq = one(diag, dq, True) * (HEAD_SIZE**-0.5)
        cosine, sine = cos_ref[:, cut], sin_ref[:, cut]
        for g in range(heads):
            a = dq[:HALF, g * size : (g + 1) * size]
            b = dq[HALF:, g * size : (g + 1) * size]
            dq_ref[0, g * HEAD_SIZE : g * HEAD_SIZE + HALF, cut] = (a * cosine + b * sine).astype(BF16)
            dq_ref[0, g * HEAD_SIZE + HALF : (g + 1) * HEAD_SIZE, cut] = (b * cosine - a * sine).astype(BF16)
    for j in range(sums.shape[0]):
        for k in range(2):
            dkv_ref[j, 0, k, 0] = sums[j, k].astype(BF16)


def attention_specs(seqs, span, all_tiles, heads_kv, heads, size):
    wide = pl.BlockSpec((1, heads * HEAD_SIZE, span), lambda s, h, b: (s, h, 0))
    kv = pl.BlockSpec((all_tiles, 1, 2, 1, HEAD_SIZE, size), lambda s, h, b: (0, s, 0, h, 0, 0))
    rows = pl.BlockSpec((1, 2, span), lambda s, h, b: (s, 0, 0))
    lse = pl.BlockSpec((1, 1, heads, span), lambda s, h, b: (s, h, 0, 0))
    table = pl.BlockSpec((HALF, span), lambda s, h, b: (0, 0))
    return wide, kv, rows, lse, table


def attend(q, kv, rows, bounds, heads):
    seqs, features, span = q.shape
    all_tiles, _, _, heads_kv, _, size = kv.shape
    wide, kvs, rs, lse, _ = attention_specs(seqs, span, all_tiles, heads_kv, heads, size)
    return pl.pallas_call(
        functools.partial(attend_kernel, heads, size),
        grid_spec=pltpu.PrefetchScalarGridSpec(
            num_scalar_prefetch=1, grid=(seqs, heads_kv), in_specs=[wide, kvs, rs], out_specs=[wide, lse]
        ),
        out_shape=[jax.ShapeDtypeStruct(q.shape, BF16), jax.ShapeDtypeStruct((seqs, heads_kv, heads, span), F32)],
        compiler_params=pltpu.CompilerParams(vmem_limit_bytes=40 << 20),
        cost_estimate=pl.CostEstimate(flops=4 * seqs * features * span * span * 3, bytes_accessed=8 << 20, transcendentals=0),
        name="attend",
    )(bounds, q, kv, rows)


def attend_back(q, kv, rows, bounds, o, do, lse, cosine, sine, heads):
    seqs, features, span = q.shape
    all_tiles, _, _, heads_kv, _, size = kv.shape
    wide, kvs, rs, ls, table = attention_specs(seqs, span, all_tiles, heads_kv, heads, size)
    return pl.pallas_call(
        functools.partial(back_kernel, heads, size),
        grid_spec=pltpu.PrefetchScalarGridSpec(
            num_scalar_prefetch=1,
            grid=(seqs, heads_kv),
            in_specs=[wide, kvs, rs, wide, wide, ls, table, table],
            out_specs=[wide, kvs],
            scratch_shapes=[pltpu.VMEM((all_tiles, 2, HEAD_SIZE, size), F32)],
        ),
        out_shape=[jax.ShapeDtypeStruct(q.shape, BF16), jax.ShapeDtypeStruct(kv.shape, BF16)],
        compiler_params=pltpu.CompilerParams(vmem_limit_bytes=40 << 20),
        cost_estimate=pl.CostEstimate(flops=10 * seqs * features * span * span * 3, bytes_accessed=16 << 20, transcendentals=0),
        name="attend_back",
    )(bounds, q, kv, rows, o, do, lse, cosine, sine)


def gather_all(shard):
    whole = lax.all_gather(shard, ("ctx", "dp"), axis=0, tiled=True)
    return whole.reshape(lax.axis_size("ctx"), -1, shard.shape[1])


def scatter_all(terms):
    flat = terms.reshape(-1, terms.shape[2])
    return lax.psum_scatter(flat, ("ctx", "dp"), scatter_dimension=0, tiled=True).astype(F32)


def norm_back(dnorm, value, scale, gain):
    dgain = jnp.sum(dnorm * value * scale, axis=(0, 1))
    scaled = dnorm * gain
    dvalue = scale * (scaled - value * scale * scale * jnp.mean(scaled * value, axis=-1, keepdims=True))
    return (dvalue, dgain)


def ein(form, left, right):
    return jnp.einsum(form, left, right, preferred_element_type=F32)


def columns_of(blocks):
    return blocks.transpose(1, 0, 2).reshape(blocks.shape[1], -1)


def body(
    tokens, segments, cotangent, attn_gain, query_weight, key_matrix, value_matrix, output_weight, second_gain,
    gate_weight, up_weight, down_weight,
):
    parts = lax.axis_size("ctx")
    seqs, span, width = tokens.shape
    nq, nk = query_weight.shape[1], key_matrix.shape[1]
    nf = gate_weight.shape[1]
    heads_kv = nk * parts // HEAD_SIZE
    heads_q = nq * parts // HEAD_SIZE
    heads = heads_q // heads_kv
    size = math.gcd(span, 256)
    tiles = span // size

    gains = lax.all_gather(jnp.stack([attn_gain, second_gain]), "ctx", axis=1, tiled=True).astype(F32)
    segs_all = lax.all_gather(segments, "ctx", axis=1, tiled=True)
    first_weights = gather_all(jnp.concatenate([query_weight, key_matrix, value_matrix, output_weight], axis=1))
    pair_shard, down_shard, first_weights = lax.optimization_barrier(
        (jnp.concatenate([gate_weight, up_weight], axis=1), down_weight, first_weights)
    )
    pair = gather_all(pair_shard)
    down = gather_all(down_shard)
    gain_one, gain_two = gains[0], gains[1]

    q_full = columns_of(first_weights[:, :, :nq])
    k_full = columns_of(first_weights[:, :, nq : nq + nk])
    v_full = columns_of(first_weights[:, :, nq + nk : nq + 2 * nk])
    o_full = columns_of(first_weights[:, :, nq + 2 * nk :])

    first = lax.axis_index("ctx") * span
    cosine, sine = rope_tables(first, span)
    place = first + jnp.arange(span, dtype=jnp.int32)
    start = jnp.sum((segs_all[:, None, :] < segments[:, :, None]).astype(jnp.int32), axis=2)
    rows = jnp.stack([start, jnp.broadcast_to(place[None], start.shape)], axis=1)
    diag = place[::size] // size
    lo = start[:, ::size] // size
    mid = jnp.minimum((start[:, size - 1 :: size] + size - 1) // size, diag[None])
    bounds = jnp.stack([lo, mid, jnp.broadcast_to(diag[None], lo.shape)], axis=2).reshape(-1)

    inputs = tokens.astype(F32)
    scale_one = lax.rsqrt(jnp.mean(inputs * inputs, axis=-1, keepdims=True) + 1e-05)
    hidden_one = (inputs * scale_one * gain_one).astype(BF16)
    key = rotate_rows(ein("df,scd->sfc", k_full, hidden_one), cosine, sine).astype(BF16)
    value = ein("df,scd->sfc", v_full, hidden_one).astype(BF16)
    kv_own = jnp.concatenate([key, value], axis=1).reshape(seqs, 2 * heads_kv * HEAD_SIZE, tiles, size)
    kv_own = kv_own.transpose(2, 0, 1, 3)
    kv = lax.all_gather(kv_own, "ctx", axis=0, tiled=True)
    kv = kv.reshape(parts * tiles, seqs, 2, heads_kv, HEAD_SIZE, size)
    query = rotate_rows(ein("df,scd->sfc", q_full, hidden_one), cosine, sine).astype(BF16)

    attended, lse = attend(query, kv, rows, bounds, heads)

    after = inputs + ein("sfc,fd->scd", attended, o_full)
    scale_two = lax.rsqrt(jnp.mean(after * after, axis=-1, keepdims=True) + 1e-05)
    hidden_two = (after * scale_two * gain_two).astype(BF16)
    g_full = columns_of(pair[:, :, :nf])
    u_full = columns_of(pair[:, :, nf:])
    d_full = columns_of(down)
    gate = ein("scd,df->scf", hidden_two, g_full)
    upward = ein("scd,df->scf", hidden_two, u_full)
    sigma = jax.nn.sigmoid(gate)
    active = gate * sigma
    inner = (active * upward).astype(BF16)
    block_output = (after + ein("scf,fd->scd", inner, d_full)).astype(BF16)

    grad_low = cotangent.astype(BF16)
    grad_parts = grad_low.reshape(seqs, span, parts, width // parts)
    down_grad = scatter_all(ein("scf,scod->ofd", inner, grad_parts).astype(BF16))
    dinner = ein("scd,fd->scf", grad_low, d_full)
    dgate = (dinner * upward * sigma * (1.0 + gate * (1.0 - sigma))).astype(BF16)
    dup = (dinner * active).astype(BF16)
    gate_term = ein("scd,scof->odf", hidden_two, dgate.reshape(seqs, span, parts, nf)).astype(BF16)
    up_term = ein("scd,scof->odf", hidden_two, dup.reshape(seqs, span, parts, nf)).astype(BF16)
    dhidden_two = ein("scf,df->scd", dgate, g_full) + ein("scf,df->scd", dup, u_full)
    dnorm_two, second_term = norm_back(dhidden_two, after, scale_two, gain_two)
    dafter = cotangent + dnorm_two
    dattn = dafter.astype(BF16)
    dattn_parts = dattn.reshape(seqs, span, parts, width // parts)
    output_term = ein("sfc,scod->ofd", attended, dattn_parts).astype(BF16)
    wide_grads = scatter_all(jnp.concatenate([gate_term, up_term, output_term], axis=2))
    gate_grad, up_grad, output_grad = wide_grads[:, :nf], wide_grads[:, nf : 2 * nf], wide_grads[:, 2 * nf :]

    dattended = ein("fd,scd->sfc", o_full, dattn).astype(BF16)
    dquery, dkv = attend_back(query, kv, rows, bounds, attended, dattended, lse, cosine, sine, heads)
    dkv = dkv.reshape(parts * tiles, seqs, 2 * heads_kv * HEAD_SIZE, size)
    dkv = lax.psum_scatter(dkv, "ctx", scatter_dimension=0, tiled=True).astype(F32)
    dkv = dkv.transpose(1, 2, 0, 3).reshape(seqs, 2 * heads_kv * HEAD_SIZE, span)
    dkey = rotate_rows(dkv[:, : heads_kv * HEAD_SIZE], cosine, -sine).astype(BF16)
    dvalue = dkv[:, heads_kv * HEAD_SIZE :].astype(BF16)
    dhidden_one = ein("sfc,df->scd", dquery, q_full)
    dhidden_one = dhidden_one + ein("sfc,df->scd", dkey, k_full)
    dhidden_one = dhidden_one + ein("sfc,df->scd", dvalue, v_full)
    stacked = jnp.concatenate(
        [
            dquery.reshape(seqs, parts, nq, span),
            dkey.reshape(seqs, parts, nk, span),
            dvalue.reshape(seqs, parts, nk, span),
        ],
        axis=2,
    )
    first_grads = scatter_all(ein("scd,sofc->odf", hidden_one, stacked).astype(BF16))
    query_grad, key_grad, value_grad = first_grads[:, :nq], first_grads[:, nq : nq + nk], first_grads[:, nq + nk :]
    dnorm_one, first_term = norm_back(dhidden_one, inputs, scale_one, gain_one)
    input_grad = dafter + dnorm_one
    gain_sums = lax.psum(jnp.stack([first_term, second_term]), ("dp", "ctx"))
    own = lax.dynamic_slice_in_dim(gain_sums, lax.axis_index("ctx") * attn_gain.shape[0], attn_gain.shape[0], axis=1)
    return (
        block_output, input_grad, own[0], query_grad, key_grad, value_grad, output_grad, own[1],
        gate_grad, up_grad, down_grad,
    )


def solution(mesh):
    three, two, one = P("dp", "ctx", None), P("dp", "ctx"), P("ctx")
    return jax.shard_map(
        body,
        mesh=mesh,
        in_specs=(three, two, three, one, two, two, two, two, one, two, two, two),
        out_specs=(three, three, one, two, two, two, two, one, two, two, two),
        check_vma=False,
    )
```

time: 1620 us -> 970 us (0.60)
  waiting for transfers between devices: 1040 us -> 585 us
  matrix products: 254 us -> 123 us
  blocking collectives: 161 us -> 48.1 us
  Pallas kernels: 0 us -> 45.5 us
  local copies, waits for them, and re-layouts: 77.7 us -> 119 us
  other arithmetic: 50.6 us -> 29.1 us
    reduce_scatter x9 -> x2, waiting for transfers between devices: 701 us -> 239 us  [the longest x1 152 us: scatter_all(): lax.psum_scatter(flat, ('ctx', 'dp'), scatter_dimension=0, tiled=True)]
    dot_general x35 -> x19, matrix products: 254 us -> 123 us  [ein(): return jnp.einsum(form, left, right, preferred_element_type=F32)]
    all_gather x10 -> x2, blocking collectives: 128 us -> 11.2 us  [the longest x1 5.98 us: body(): lax.all_gather(jnp.stack([attn_gain, second_gain]), 'ctx', axis=1, tiled=...]
    pallas_call x0 -> x2, Pallas kernels: none -> 45.5 us  [the longest x1 26 us: attend_back(): pl.pallas_call(functools.partial(back_kernel, heads, size), grid_spec=plt...]
    all_gather x7 -> x4, waiting for transfers between devices: 163 us -> 195 us  [the longest x3 175 us: gather_all(): whole = lax.all_gather(shard, ('ctx', 'dp'), axis=0, tiled=True)]
    transpose x0 -> x1, local copies, waits for them, and re-layouts: none -> 31.1 us  [columns_of(): return blocks.transpose(1, 0, 2).reshape(blocks.shape[1], -1)]
    reshape x1 -> x6, local copies, waits for them, and re-layouts: 2.11 us -> 28.8 us  [the longest x2 18.4 us: columns_of(): return blocks.transpose(1, 0, 2).reshape(blocks.shape[1], -1)]
    unnamed x28 -> x10, waiting for transfers between devices: 170 us -> 151 us
  transfers between devices with their start and end apart: 22 -> 8, of which waited for: 16 -> 8; matrix products, arithmetic and copies ran while one was open for 15% -> 12% of each run, Pallas kernels for 0% -> 2%
where the time goes in v1:
time: 970 us; the launch traced here: 964 us
  waiting for transfers between devices  585 us (60%)
  matrix products  123 us (13%)
  local copies, waits for them, and re-layouts  119 us (12%)
  blocking collectives  48.1 us (5%)
  Pallas kernels  45.5 us (5%)
  other arithmetic  29.1 us (3%)
  between operations  15.2 us (2%)
    all_gather x3, waiting for transfers between devices, gather_all(): whole = lax.all_gather(shard, ('ctx', 'dp'), axis=0, tiled=True)  175 us
    reduce_scatter x1, waiting for transfers between devices, scatter_all(): lax.psum_scatter(flat, ('ctx', 'dp'), scatter_dimension=0, tiled=True)  152 us
    unnamed x10, waiting for transfers between devices  151 us
    dot_general x19, matrix products, ein(): return jnp.einsum(form, left, right, preferred_element_type=F32)  123 us
    reduce_scatter x1, waiting for transfers between devices, body(): lax.psum_scatter(dkv, 'ctx', scatter_dimension=0, tiled=True).astype(F32)  87.2 us
    psum x1, blocking collectives, body(): gain_sums = lax.psum(jnp.stack([first_term, second_term]), ('dp', 'ctx'))  37 us
    transpose x1, local copies, waits for them, and re-layouts, columns_of(): return blocks.transpose(1, 0, 2).reshape(blocks.shape[1], -1)  31.1 us
    unnamed x80, local copies, waits for them, and re-layouts  30.6 us
  transfers between devices with their start and end apart: 8, of which 8 were waited for; matrix products, arithmetic and copies ran while one was open for 12% of the time, Pallas kernels for 2%

profile of v1, /device:TPU:0, one launch (start us, length us, event | category | flops | bytes accessed | tf_op | source)
XLA Modules:
  0.0 964.4 jit_solution(14738754116045864843)
XLA Ops:
  22.8 55.8 %all-gather.6.cloned.1.call-done = bf16[3840,640]{1,0:T(8,128)(2,1)} async-done(((bf16[120,640]{1,0:T(8,128)(2,1)}), bf16[3840,640]{1,0:T(8,128)(2,1)}) %all-gather.6.cloned.1.call-update) | async-done | bytes 4915216 | tf_op jit(solution)/shard_map/all_gather | solution.py:167
  78.5 8.1 copy.158
  110.8 20.2 %all-gather.8.cloned.1.call-done = bf16[8,2,640,256]{3,2,1,0:T(8,128)(2,1)} async-done(((bf16[2,2,640,256]{3,2,1,0:T(8,128)(2,1)}), bf16[8,2,640,256]{3,2,1,0:T(8,128)(2,1)}) %all-gather.8.cloned.1.call-update) | async-done | bytes 5242896 | tf_op jit(solution)/shard_map/all_gather | solution.py:237
  133.5 19.5 %attend.1 = (bf16[2,960,512]{2,1,0:T(8,128)(2,1)S(1)}, f32[2,5,3,512]{3,2,1,0:T(4,128)S(1)}) custom-call(s32[12]{0:T(128)S(1)} %reshape.244.bounds, bf16[2,960,512]{2,1,0:T(8,128)(2,1)S(1)} %bitcast.201, bf16[8,2,2,5,64,256]{5,4,3,2,1,0:T(8,128)(2,1)S(1)} %bitcast.204, s32[2,2,512]{2,1,0:T(2,128)S(1)} %pad_add_fusion.rows_ref), custom_call_target="tpu_custom_call" | custom-call | flops 6039797760 | bytes 8388608 | tf_op jit(solution)/shard_map/attend/pallas_call | solution.py:134
  158.9 41.2 %all-gather.12.cloned.1.call-done = bf16[10240,240]{1,0:T(8,128)(2,1)} async-done(((bf16[320,240]{1,0:T(8,128)(2,1)}), bf16[10240,240]{1,0:T(8,128)(2,1)}) %all-gather.12.cloned.1.call-update) | async-done | bytes 4915216 | tf_op jit(solution)/shard_map/all_gather | solution.py:167
  207.8 77.7 %all-gather.10.cloned.1.call-done = bf16[3840,1280]{1,0:T(8,128)(2,1)} async-done(((bf16[120,1280]{1,0:T(8,128)(2,1)}), bf16[3840,1280]{1,0:T(8,128)(2,1)}) %all-gather.10.cloned.1.call-update) | async-done | bytes 9830416 | tf_op jit(solution)/shard_map/all_gather | solution.py:167
  285.6 8.3 fusion.61
  293.9 31.1 %copy_bitcast_fusion = (bf16[960,4,640]{2,1,0:T(4,128)(2,1)}, bf16[960,4,640]{2,1,0:T(4,128)(2,1)}) fusion(bf16[4,960,640]{2,1,0:T(8,128)(2,1)} %get-tuple-element.101, bf16[4,960,640]{2,1,0:T(8,128)(2,1)} %get-tuple-element.100), kind=kLoop, calls=%fused_computation.29 | loop fusion | bytes 19660800 | tf_op jit(solution)/shard_map/transpose | solution.py:188
  325.0 9.4 reshape.282
  334.4 9.0 reshape.281
  343.4 10.7 %fusion.70 = f32[2,512,2560]{2,1,0:T(8,128)} fusion(bf16[2,512,960]{1,2,0:T(8,128)(2,1)} %multiply_convert_fusion.1, bf16[960,2560,1]{1,0,2:T(8,128)(2,1)} %reshape.282), kind=kOutput, calls=%fused_computation.124 | convolution fusion | flops 5033164800 | bytes 17367040 | tf_op jit(solution)/shard_map/scd,df->scf/dot_general | solution.py:184
  354.1 8.3 fusion.69
  362.3 20.5 %fusion.3 = (bf16[2,512,2560]{2,1,0:T(8,128)(2,1)}, bf16[2,512,2560]{2,1,0:T(8,128)(2,1)}, bf16[2,512,2560]{2,1,0:T(8,128)(2,1)}) fusion(f32[2,512,2560]{2,1,0:T(8,128)} %fusion.69, f32[2,512,2560]{2,1,0:T(8,128)} %fusion.70, bf16[2560,960,1]{0,1,2:T(8,128)(2,1)} %bitcast.215, bf16[2,512,960]{1,2,0:T(8,128)(2,1)} %convert_element_type.135), kind=kOutput, calls=%fused_computation.6 | convolution fusion | flops 5072486400 | bytes 43581440 | tf_op jit(solution)/shard_map/scd,fd->scf/dot_general | solution.py:184
  382.8 9.2 fusion.71
  392.0 9.0 multiply_reduce_fusion
  406.3 26.0 %attend_back.1 = (bf16[2,960,512]{2,1,0:T(8,128)(2,1)S(1)}, bf16[8,2,2,5,64,256]{5,4,3,2,1,0:T(8,128)(2,1)S(1)}) custom-call(s32[12]{0:T(128)S(1)} %reshape.244.bounds, bf16[2,960,512]{2,1,0:T(8,128)(2,1)S(1)} %bitcast.202, bf16[8,2,2,5,64,256]{5,4,3,2,1,0:T(8,128)(2,1)} %bitcast.203, s32[2,2,512]{2,1,0:T(2,128)S(1)} %pad_add_fusion.rows_ref, ...), custom_call_target="tpu_custom_call" | custom-call | flops 15099494400 | bytes 16777216 | tf_op jit(solution)/shard_map/attend_back/pallas_call | solution.py:150
  437.5 9.4 fusion.14
  454.8 87.2 %reduce-scatter.9.cloned.1.call-done = bf16[2,2,640,256]{3,2,1,0:T(8,128)(2,1)} async-done(((bf16[8,2,640,256]{3,2,1,0:T(8,128)(2,1)}), bf16[2,2,640,256]{3,2,1,0:T(8,128)(2,1)}) %reduce-scatter.9.cloned.1.call-update) | async-done | bytes 1310736 | tf_op jit(solution)/shard_map/reduce_scatter | solution.py:276
  561.6 8.3 fusion.12
  586.4 9.8 %add_convert_fusion = bf16[2,512,960]{1,2,0:T(8,128)(2,1)} fusion(f32[2,512,960]{1,2,0:T(8,128)S(1)} %copy-done.13, bf16[2,512,2560]{2,1,0:T(8,128)(2,1)} %get-tuple-element.99, bf16[2560,960,1]{0,1,2:T(8,128)(2,1)} %bitcast.216), kind=kOutput, calls=%fused_computation.48 | convolution fusion | flops 5035130880 | bytes 16056320 | tf_op jit(solution)/shard_map/scf,fd->scd/dot_general | solution.py:184
  596.1 95.2 %reduce-scatter.15.cloned.1.call-done = bf16[320,240]{1,0:T(8,128)(2,1)} async-done(((bf16[10240,240]{1,0:T(8,128)(2,1)}), bf16[320,240]{1,0:T(8,128)(2,1)}) %reduce-scatter.15.cloned.1.call-update) | async-done | bytes 153616
  701.1 37.0 %psum.7 = f32[2,960]{1,0:T(2,128)S(1)} all-reduce(f32[2,960]{1,0:T(2,128)S(1)} %pad_maximum_fusion.6), channel_id=1, replica_groups=mesh['dp'=8,'ctx'=4] {'dp','ctx'}, use_global_device_ids=true, to_apply=%region_8.9 | all-reduce | flops 1920 | bytes 15360 | tf_op jit(solution)/shard_map/psum | solution.py:295
  745.0 54.6 %reduce-scatter.13.cloned.1.call-done = bf16[120,400]{1,0:T(8,128)(2,1)} async-done(((bf16[3840,400]{1,0:T(8,128)(2,1)}), bf16[120,400]{1,0:T(8,128)(2,1)}) %reduce-scatter.13.cloned.1.call-update) | async-done | bytes 96016
  802.0 151.8 %reduce-scatter.11.cloned.1.call-done = bf16[120,1520]{1,0:T(8,128)(2,1)} async-done(((bf16[3840,1520]{1,0:T(8,128)(2,1)}), bf16[120,1520]{1,0:T(8,128)(2,1)}) %reduce-scatter.11.cloned.1.call-update) | async-done | bytes 364816 | tf_op jit(solution)/shard_map/reduce_scatter | solution.py:173
  (165 shorter events, 132.2 us)
Async XLA Ops:
  7.2 71.4 %all-gather.6.cloned.1.call-start = ((), (), s32[]{:S(2)}) async-start(), calls=%async_computation.4 | async-start | bytes 5068800 | tf_op jit(solution)/shard_map/all_gather | solution.py:167
  10.6 120.4 %all-gather.8.cloned.1.call-start = ((), (), s32[]{:S(2)}) async-start(), calls=%async_computation.5 | async-start | bytes 6553600 | tf_op jit(solution)/shard_map/all_gather | solution.py:237
  20.0 87.6 %copy-start.27 = (f32[2,512]{1,0:T(2,128)}, f32[2,512]{1,0:T(2,128)S(1)}, u32[]{:S(2)}) copy-start(f32[2,512]{1,0:T(2,128)S(1)} %add_rsqrt_fusion.1) | copy-start | bytes 12292
  20.1 87.5 %copy-start.29 = (f32[1,960]{1,0:T(1,128)}, f32[1,960]{1,0:T(1,128)S(1)}, u32[]{:S(2)}) copy-start(f32[1,960]{1,0:T(1,128)S(1)} %get-tuple-element.121) | copy-start | bytes 11524
  78.5 9.5 copy-start.6
  91.6 108.5 %all-gather.12.cloned.1.call-start = ((), (), s32[]{:S(2)}) async-start(), calls=%async_computation.7 | async-start | bytes 5406720 | tf_op jit(solution)/shard_map/all_gather | solution.py:167
  92.4 193.2 %all-gather.10.cloned.1.call-start = ((), (), s32[]{:S(2)}) async-start(), calls=%async_computation.6 | async-start | bytes 10137600 | tf_op jit(solution)/shard_map/all_gather | solution.py:167
  92.9 449.0 %reduce-scatter.9.cloned.1.call-start = ((), (), s32[]{:S(2)}) async-start(), calls=%async_computation.8 | async-start | bytes 6553600 | tf_op jit(solution)/shard_map/reduce_scatter | solution.py:276
  133.5 19.5 %copy-start.7 = (bf16[2,512,960]{1,2,0:T(8,128)(2,1)S(1)}, bf16[2,512,960]{1,2,0:T(8,128)(2,1)}, u32[]{:S(2)}) copy-start(bf16[2,512,960]{1,2,0:T(8,128)(2,1)} %param.12) | copy-start | bytes 5898244
  133.5 19.5 %copy-start.24 = (bf16[4,960,240]{1,2,0:T(8,128)(2,1)S(1)}, bf16[4,960,240]{1,2,0:T(8,128)(2,1)}, u32[]{:S(2)}) copy-start(bf16[4,960,240]{1,2,0:T(8,128)(2,1)} %get-tuple-element.105) | copy-start | bytes 5529604
  343.4 10.7 %copy-start.14 = (bf16[960,2560,1]{1,0,2:T(8,128)(2,1)S(1)}, bf16[960,2560,1]{1,0,2:T(8,128)(2,1)}, u32[]{:S(2)}) copy-start(bf16[960,2560,1]{1,0,2:T(8,128)(2,1)} %reshape.281) | copy-start | bytes 14745604
  343.4 10.7 %copy-start.19 = (bf16[2,512,960]{1,2,0:T(8,128)(2,1)S(1)}, bf16[2,512,960]{1,2,0:T(8,128)(2,1)}, u32[]{:S(2)}) copy-start(bf16[2,512,960]{1,2,0:T(8,128)(2,1)} %multiply_convert_fusion.1) | copy-start | bytes 5898244
  382.8 9.2 copy-start.12
  382.8 9.2 copy-start.33
  392.0 9.0 copy-start.10
  435.9 255.4 %reduce-scatter.15.cloned.1.call-start = ((), (), s32[]{:S(2)}) async-start(), calls=%async_computation.11 | async-start | bytes 5406720
  454.7 89.0 %copy-start.26 = (f32[32,512]{1,0:T(8,128)S(1)}, f32[32,512]{1,0:T(8,128)}, u32[]{:S(2)}) copy-start(f32[32,512]{1,0:T(8,128)} %get-tuple-element.122) | copy-start | bytes 196612
  454.7 344.9 %reduce-scatter.13.cloned.1.call-start = ((), (), s32[]{:S(2)}) async-start(), calls=%async_computation.10 | async-start | bytes 4055040
  557.0 396.9 %reduce-scatter.11.cloned.1.call-start = ((), (), s32[]{:S(2)}) async-start(), calls=%async_computation.9 | async-start | bytes 12165120 | tf_op jit(solution)/shard_map/reduce_scatter | solution.py:173
  557.0 12.9 %slice-start = ((s8[5242880]{0:T(1024)(128)(4,1)}), s8[4194304]{0:T(1024)(128)(4,1)S(1)}, s32[]{:S(2)}) async-start(s8[5242880]{0:T(1024)(128)(4,1)} %bitcast.250), calls=%async_computation.12 | async-start | bytes 8388608
  561.6 8.3 slice-start.1
  580.5 5.9 copy-start.13
  596.1 99.8 %copy-start.9 = (bf16[2,512,960]{1,2,0:T(8,128)(2,1)S(1)}, bf16[2,512,960]{1,2,0:T(8,128)(2,1)}, u32[]{:S(2)}) copy-start(bf16[2,512,960]{1,2,0:T(8,128)(2,1)} %param.12) | copy-start | bytes 5898244
  696.0 5.1 copy-start.32
  (20 other events, 45.2 us)
Sparse Core Ops, SparseCore 0:
  11.4 67.0 all-gather.5
  91.7 39.2 all-gather.7
  133.9 66.1 all-gather.11
  203.4 82.1 all-gather.9
  436.1 105.8 reduce-scatter.8
  544.2 147.1 reduce-scatter.14
  697.6 101.9 reduce-scatter.12
  806.7 147.0 reduce-scatter.10

commit v2 on v1

--- a/solution.py
+++ b/solution.py
@@ -158,7 +158,7 @@
         ),
         out_shape=[jax.ShapeDtypeStruct(q.shape, BF16), jax.ShapeDtypeStruct(kv.shape, BF16)],
         compiler_params=pltpu.CompilerParams(vmem_limit_bytes=40 << 20),
-        cost_estimate=pl.CostEstimate(flops=10 * seqs * features * span * span * 3, bytes_accessed=16 << 20, transcendentals=0),
+        cost_estimate=pl.CostEstimate(flops=seqs * features * span, bytes_accessed=1 << 20, transcendentals=0),
         name="attend_back",
     )(bounds, q, kv, rows, o, do, lse, cosine, sine)
 
@@ -171,6 +171,235 @@
 def scatter_all(terms):
     flat = terms.reshape(-1, terms.shape[2])
     return lax.psum_scatter(flat, ("ctx", "dp"), scatter_dimension=0, tiled=True).astype(F32)
+
+
+def bits_of(axis):
+    return lax.axis_size(axis).bit_length() - 1
+
+
+def all_places():
+    return [(axis, bit) for axis in ("ctx", "dp") for bit in reversed(range(bits_of(axis)))]
+
+
+def doubling_order(flip):
+    high = [("dp", bit) for bit in reversed(range(1, bits_of("dp")))]
+    low = [("dp", 0)]
+    across = [("ctx", bit) for bit in reversed(range(1, bits_of("ctx")))]
+    return high + (across + low if flip else low + across) + [("ctx", 0)]
+
+
+def partners(axis, bit):
+    return [(i, i ^ (1 << bit)) for i in range(lax.axis_size(axis))]
+
+
+def side_of(axis, bit):
+    return (lax.axis_index(axis) >> bit) & 1
+
+
+def join(mine, other, side, at):
+    low = jnp.where(side == 0, mine, other)
+    high = jnp.where(side == 0, other, mine)
+    return jnp.stack([low, high], axis=at)
+
+
+def gather_doubling(shard, flip):
+    places, held, value = all_places(), [], shard
+    for place in doubling_order(flip):
+        other = lax.ppermute(value, place[0], partners(*place))
+        at = sum(places.index(h) < places.index(place) for h in held)
+        value = join(value, other, side_of(*place), at)
+        held.append(place)
+    return value.reshape(lax.axis_size("ctx"), -1, shard.shape[1])
+
+
+def halve(value, left, place):
+    at, side = left.index(place), side_of(*place)
+    away = lax.dynamic_index_in_dim(value, 1 - side, at, keepdims=False)
+    kept = lax.dynamic_index_in_dim(value, side, at, keepdims=False)
+    left.remove(place)
+    return kept + lax.ppermute(away, place[0], partners(*place))
+
+
+def halve_first(terms, flip, steps):
+    left, order = all_places(), doubling_order(flip)[::-1]
+    value = terms.reshape((2,) * len(left) + (-1, terms.shape[2]))
+    for place in order[:steps]:
+        value = halve(value, left, place)
+    return value
+
+
+def halve_rest(value, flip, steps):
+    order = doubling_order(flip)[::-1]
+    left = [place for place in all_places() if place not in order[:steps]]
+    for place in order[steps:]:
+        value = halve(value, left, place)
+    return value.astype(F32)
+
+
+def earlier_blocks(own, *later):
+    value, held = own, 0
+    for bit in reversed(range(bits_of("ctx"))):
+        pairs = partners("ctx", bit)
+        if held == 0 and bit > 0:
+            pairs = [(i, j) for i, j in pairs if i < j]
+        other = lax.ppermute(value, "ctx", pairs)
+        if held == 0:
+            other, *later = lax.optimization_barrier((other, *later))
+        value = join(value, other, side_of("ctx", bit), held)
+        held += 1
+    return (value.reshape((-1,) + own.shape), *later)
+
+
+def owners_sum(blocks, *later):
+    left = [("ctx", bit) for bit in reversed(range(bits_of("ctx")))]
+    value = blocks.reshape((2,) * len(left) + blocks.shape[1:])
+    for place in left[::-1]:
+        pairs, first = partners(*place), place[1] == 0
+        if len(left) == 1 and not first:
+            pairs = [(i, j) for i, j in pairs if i > j]
+        at, side = left.index(place), side_of(*place)
+        away = lax.dynamic_index_in_dim(value, 1 - side, at, keepdims=False)
+        kept = lax.dynamic_index_in_dim(value, side, at, keepdims=False)
+        value = kept + lax.ppermute(away, "ctx", pairs)
+        left.remove(place)
+        if first:
+            value, *later = lax.optimization_barrier((value, *later))
+    return (value, *later)
+
+
+def every_block(own):
+    value = own
+    for held, bit in enumerate(reversed(range(bits_of("ctx")))):
+        value = join(value, lax.ppermute(value, "ctx", partners("ctx", bit)), side_of("ctx", bit), held)
+    return value.reshape((-1,) + own.shape)
+
+
+def sum_everywhere(value):
+    for place in all_places():
+        value = value + lax.ppermute(value, place[0], partners(*place))
+    return value
+
+
+def term_kernel(left_ref, right_ref, out_ref):
+    seqs, features, _ = left_ref.shape
+    lines = math.gcd(features, 192)
+
+    def some_rows(k, carry):
+        cut = pl.ds(pl.multiple_of(k * lines, lines), lines)
+        total = contract(left_ref[0, cut, :], right_ref[0, 0], (1, 1))
+        for s in range(1, seqs):
+            total += contract(left_ref[s, cut, :], right_ref[s, 0], (1, 1))
+        out_ref[0, cut, :] = total.astype(BF16)
+        return carry
+
+    lax.fori_loop(0, features // lines, some_rows, 0)
+
+
+def weight_term(left, right):
+    seqs, features, span = left.shape
+    _, parts, columns, _ = right.shape
+    return pl.pallas_call(
+        term_kernel,
+        grid=(parts,),
+        in_specs=[
+            pl.BlockSpec((seqs, features, span), lambda p: (0, 0, 0)),
+            pl.BlockSpec((seqs, 1, columns, span), lambda p: (0, p, 0, 0)),
+        ],
+        out_specs=pl.BlockSpec((1, features, columns), lambda p: (p, 0, 0)),
+        out_shape=jax.ShapeDtypeStruct((parts, features, columns), BF16),
+        compiler_params=pltpu.CompilerParams(vmem_limit_bytes=24 << 20),
+        cost_estimate=pl.CostEstimate(flops=2 * seqs * span * features, bytes_accessed=1 << 20, transcendentals=0),
+        name="weight_term",
+    )(left, right)
+
+
+def ffn_kernel(nf, h_ref, ht_ref, gb_ref, after_ref, pair_ref, d_ref, y_ref, dh_ref, pg_ref, dg_ref, dfull, hid, dgate, dup, yacc):
+    c = pl.program_id(0)
+    count, width = h_ref.shape
+    parts = d_ref.shape[0]
+    nd = d_ref.shape[2]
+
+    @pl.when(c == 0)
+    def _():
+        yacc[...] = after_ref[...]
+        dh_ref[...] = jnp.zeros_like(dh_ref)
+
+    dfull[...] = jnp.concatenate([d_ref[o] for o in range(parts)], axis=1)
+    step = math.gcd(count, 256)
+
+    def token_rows(r, carry):
+        cut = pl.ds(pl.multiple_of(r * step, step), step)
+        h, gb = h_ref[cut, :], gb_ref[cut, :]
+        g, u = pair_ref[0, :, :nf], pair_ref[0, :, nf : 2 * nf]
+        gate = contract(h, g, (1, 0))
+        up = contract(h, u, (1, 0))
+        dhid = contract(gb, dfull[...], (1, 1))
+        sg = 1.0 / (1.0 + jnp.exp(-gate))
+        active = gate * sg
+        low = (active * up).astype(BF16)
+        hid[cut, :] = low
+        yacc[cut, :] += contract(low, dfull[...], (1, 0))
+        dg = (dhid * up * sg * (1.0 + gate * (1.0 - sg))).astype(BF16)
+        du = (dhid * active).astype(BF16)
+        dgate[cut, :] = dg
+        dup[cut, :] = du
+        dh_ref[cut, :] += contract(dg, g, (1, 1)) + contract(du, u, (1, 1))
+        return carry
+
+    lax.fori_loop(0, count // step, token_rows, 0)
+    lines = math.gcd(width, 192)
+
+    def pair_rows(k, carry):
+        cut = pl.ds(pl.multiple_of(k * lines, lines), lines)
+        ht = ht_ref[cut, :]
+        pg_ref[0, cut, :nf] = contract(ht, dgate[...], (1, 0)).astype(BF16)
+        pg_ref[0, cut, nf:] = contract(ht, dup[...], (1, 0)).astype(BF16)
+        return carry
+
+    lax.fori_loop(0, width // lines, pair_rows, 0)
+    lanes = 128 if nf % 128 == 0 else nf
+    for k in range(nf // lanes):
+        term = contract(hid[:, k * lanes : (k + 1) * lanes], gb_ref[...], (0, 0))
+        for o in range(parts):
+            dg_ref[o, k * lanes : (k + 1) * lanes, :] = term[:, o * nd : (o + 1) * nd].astype(BF16)
+
+    @pl.when(c == parts - 1)
+    def _():
+        y_ref[...] = yacc[...].astype(BF16)
+
+
+def feed_forward(hidden, hidden_t, grad, after, pair, down, nf):
+    count, width = hidden.shape
+    parts, depth, nd = down.shape
+    whole = lambda *shape: pl.BlockSpec(shape, lambda c: (0,) * len(shape), pipeline_mode=pl.Buffered(1))
+    return pl.pallas_call(
+        functools.partial(ffn_kernel, nf),
+        grid=(parts,),
+        in_specs=[
+            whole(count, width), whole(width, count), whole(count, width), whole(count, width),
+            pl.BlockSpec((1, width, pair.shape[2]), lambda c: (c, 0, 0)),
+            pl.BlockSpec((parts, nf, nd), lambda c: (0, c, 0)),
+        ],
+        out_specs=[
+            pl.BlockSpec((count, width), lambda c: (0, 0)),
+            pl.BlockSpec((count, width), lambda c: (0, 0)),
+            pl.BlockSpec((1, width, 2 * nf), lambda c: (c, 0, 0)),
+            pl.BlockSpec((parts, nf, nd), lambda c: (0, c, 0)),
+        ],
+        out_shape=[
+            jax.ShapeDtypeStruct((count, width), BF16),
+            jax.ShapeDtypeStruct((count, width), F32),
+            jax.ShapeDtypeStruct((parts, width, 2 * nf), BF16),
+            jax.ShapeDtypeStruct((parts, depth, nd), BF16),
+        ],
+        scratch_shapes=[
+            pltpu.VMEM((nf, width), BF16), pltpu.VMEM((count, nf), BF16), pltpu.VMEM((count, nf), BF16),
+            pltpu.VMEM((count, nf), BF16), pltpu.VMEM((count, width), F32),
+        ],
+        compiler_params=pltpu.CompilerParams(vmem_limit_bytes=58 << 20),
+        cost_estimate=pl.CostEstimate(flops=18 * count * width * depth, bytes_accessed=60 << 20, transcendentals=0),
+        name="feed_forward",
+    )(hidden, hidden_t, grad, after, pair, down)
 
 
 def norm_back(dnorm, value, scale, gain):
@@ -202,20 +431,16 @@
     size = math.gcd(span, 256)
     tiles = span // size
 
-    gains = lax.all_gather(jnp.stack([attn_gain, second_gain]), "ctx", axis=1, tiled=True).astype(F32)
-    segs_all = lax.all_gather(segments, "ctx", axis=1, tiled=True)
-    first_weights = gather_all(jnp.concatenate([query_weight, key_matrix, value_matrix, output_weight], axis=1))
-    pair_shard, down_shard, first_weights = lax.optimization_barrier(
-        (jnp.concatenate([gate_weight, up_weight], axis=1), down_weight, first_weights)
-    )
-    pair = gather_all(pair_shard)
-    down = gather_all(down_shard)
+    gains = every_block(jnp.stack([attn_gain, second_gain])).transpose(1, 0, 2).reshape(2, width).astype(F32)
+    segs_all = every_block(segments).transpose(1, 0, 2).reshape(seqs, parts * span)
+    pair_shard = jnp.concatenate([gate_weight, up_weight, output_weight], axis=1)
+    down = gather_all(down_weight)
+    q_blocks = gather_doubling(query_weight, False)
+    kv_blocks = gather_doubling(jnp.concatenate([key_matrix, value_matrix], axis=1), True)
     gain_one, gain_two = gains[0], gains[1]
 
-    q_full = columns_of(first_weights[:, :, :nq])
-    k_full = columns_of(first_weights[:, :, nq : nq + nk])
-    v_full = columns_of(first_weights[:, :, nq + nk : nq + 2 * nk])
-    o_full = columns_of(first_weights[:, :, nq + 2 * nk :])
+    k_full = columns_of(kv_blocks[:, :, :nk])
+    v_full = columns_of(kv_blocks[:, :, nk:])
 
     first = lax.axis_index("ctx") * span
     cosine, sine = rope_tables(first, span)
@@ -234,46 +459,42 @@
     value = ein("df,scd->sfc", v_full, hidden_one).astype(BF16)
     kv_own = jnp.concatenate([key, value], axis=1).reshape(seqs, 2 * heads_kv * HEAD_SIZE, tiles, size)
     kv_own = kv_own.transpose(2, 0, 1, 3)
-    kv = lax.all_gather(kv_own, "ctx", axis=0, tiled=True)
+    kv, pair_shard, q_blocks = earlier_blocks(kv_own, pair_shard, q_blocks)
+    q_full = columns_of(q_blocks)
+    pair = gather_all(pair_shard)
     kv = kv.reshape(parts * tiles, seqs, 2, heads_kv, HEAD_SIZE, size)
     query = rotate_rows(ein("df,scd->sfc", q_full, hidden_one), cosine, sine).astype(BF16)
 
+    query, down = lax.optimization_barrier((query, down))
     attended, lse = attend(query, kv, rows, bounds, heads)
 
+    o_full = columns_of(pair[:, :, 2 * nf :])
     after = inputs + ein("sfc,fd->scd", attended, o_full)
     scale_two = lax.rsqrt(jnp.mean(after * after, axis=-1, keepdims=True) + 1e-05)
-    hidden_two = (after * scale_two * gain_two).astype(BF16)
-    g_full = columns_of(pair[:, :, :nf])
-    u_full = columns_of(pair[:, :, nf:])
-    d_full = columns_of(down)
-    gate = ein("scd,df->scf", hidden_two, g_full)
-    upward = ein("scd,df->scf", hidden_two, u_full)
-    sigma = jax.nn.sigmoid(gate)
-    active = gate * sigma
-    inner = (active * upward).astype(BF16)
-    block_output = (after + ein("scf,fd->scd", inner, d_full)).astype(BF16)
-
-    grad_low = cotangent.astype(BF16)
-    grad_parts = grad_low.reshape(seqs, span, parts, width // parts)
-    down_grad = scatter_all(ein("scf,scod->ofd", inner, grad_parts).astype(BF16))
-    dinner = ein("scd,fd->scf", grad_low, d_full)
-    dgate = (dinner * upward * sigma * (1.0 + gate * (1.0 - sigma))).astype(BF16)
-    dup = (dinner * active).astype(BF16)
-    gate_term = ein("scd,scof->odf", hidden_two, dgate.reshape(seqs, span, parts, nf)).astype(BF16)
-    up_term = ein("scd,scof->odf", hidden_two, dup.reshape(seqs, span, parts, nf)).astype(BF16)
-    dhidden_two = ein("scf,df->scd", dgate, g_full) + ein("scf,df->scd", dup, u_full)
+    hidden_two = (after * scale_two * gain_two).astype(BF16).reshape(seqs * span, width)
+    grad_low = cotangent.astype(BF16).reshape(seqs * span, width)
+    block_output, dhidden_two, pair_term, down_term = feed_forward(
+        hidden_two, hidden_two.T, grad_low, after.reshape(seqs * span, width), pair, down, nf
+    )
+    block_output = block_output.reshape(seqs, span, width)
+    dhidden_two = dhidden_two.reshape(seqs, span, width)
+    down_sum = halve_first(down_term, True, 1)
+    pair_grads = scatter_all(pair_term)
     dnorm_two, second_term = norm_back(dhidden_two, after, scale_two, gain_two)
     dafter = cotangent + dnorm_two
     dattn = dafter.astype(BF16)
-    dattn_parts = dattn.reshape(seqs, span, parts, width // parts)
-    output_term = ein("sfc,scod->ofd", attended, dattn_parts).astype(BF16)
-    wide_grads = scatter_all(jnp.concatenate([gate_term, up_term, output_term], axis=2))
-    gate_grad, up_grad, output_grad = wide_grads[:, :nf], wide_grads[:, nf : 2 * nf], wide_grads[:, 2 * nf :]
+    dattn_parts = dattn.transpose(0, 2, 1).reshape(seqs, parts, width // parts, span)
+    output_term = weight_term(attended, dattn_parts)
+    output_sum = halve_first(output_term, True, 1)
 
     dattended = ein("fd,scd->sfc", o_full, dattn).astype(BF16)
+    dattended, down_sum = lax.optimization_barrier((dattended, down_sum))
     dquery, dkv = attend_back(query, kv, rows, bounds, attended, dattended, lse, cosine, sine, heads)
-    dkv = dkv.reshape(parts * tiles, seqs, 2 * heads_kv * HEAD_SIZE, size)
-    dkv = lax.psum_scatter(dkv, "ctx", scatter_dimension=0, tiled=True).astype(F32)
+    hidden_one_t = hidden_one.transpose(0, 2, 1)
+    dkv, dquery_late = owners_sum(dkv.reshape(parts, tiles, seqs, 2 * heads_kv * HEAD_SIZE, size), dquery)
+    query_sum = halve_first(weight_term(hidden_one_t, dquery_late.reshape(seqs, parts, nq, span)), True, 2)
+    dkv, query_sum = lax.optimization_barrier((dkv, query_sum))
+    dkv = dkv.astype(F32)
     dkv = dkv.transpose(1, 2, 0, 3).reshape(seqs, 2 * heads_kv * HEAD_SIZE, span)
     dkey = rotate_rows(dkv[:, : heads_kv * HEAD_SIZE], cosine, -sine).astype(BF16)
     dvalue = dkv[:, heads_kv * HEAD_SIZE :].astype(BF16)
@@ -282,17 +503,24 @@
     dhidden_one = dhidden_one + ein("sfc,df->scd", dvalue, v_full)
     stacked = jnp.concatenate(
         [
-            dquery.reshape(seqs, parts, nq, span),
             dkey.reshape(seqs, parts, nk, span),
             dvalue.reshape(seqs, parts, nk, span),
         ],
         axis=2,
     )
-    first_grads = scatter_all(ein("scd,sofc->odf", hidden_one, stacked).astype(BF16))
-    query_grad, key_grad, value_grad = first_grads[:, :nq], first_grads[:, nq : nq + nk], first_grads[:, nq + nk :]
+    stacked, pair_grads = lax.optimization_barrier((stacked, pair_grads))
+    gate_grad, up_grad = pair_grads[:, :nf], pair_grads[:, nf:]
     dnorm_one, first_term = norm_back(dhidden_one, inputs, scale_one, gain_one)
+    kv_term, query_sum, down_sum, output_sum, gain_terms = lax.optimization_barrier(
+        (weight_term(hidden_one_t, stacked), query_sum, down_sum, output_sum, jnp.stack([first_term, second_term]))
+    )
+    query_grad = halve_rest(query_sum, True, 2)
+    down_grad = halve_rest(down_sum, True, 1)
+    output_grad = halve_rest(output_sum, True, 1)
+    kv_grads = halve_rest(halve_first(kv_term, False, 1), False, 1)
+    key_grad, value_grad = kv_grads[:, :nk], kv_grads[:, nk:]
     input_grad = dafter + dnorm_one
-    gain_sums = lax.psum(jnp.stack([first_term, second_term]), ("dp", "ctx"))
+    gain_sums = sum_everywhere(gain_terms)
     own = lax.dynamic_slice_in_dim(gain_sums, lax.axis_index("ctx") * attn_gain.shape[0], attn_gain.shape[0], axis=1)
     return (
         block_output, input_grad, own[0], query_grad, key_grad, value_grad, output_grad, own[1],

time: 970 us -> 614 us (0.63)
  waiting for transfers between devices: 585 us -> 193 us
  matrix products: 123 us -> 24.3 us
  Pallas kernels: 45.5 us -> 141 us
  starting transfers between devices: 0.32 us -> 77.8 us
  blocking collectives: 48.1 us -> 0 us
  other arithmetic: 29.1 us -> 63.6 us
  local copies, waits for them, and re-layouts: 119 us -> 89.5 us
    reduce_scatter x1, waiting for transfers between devices: 152 us -> 0.01 us  [scatter_all(): lax.psum_scatter(flat, ('ctx', 'dp'), scatter_dimension=0, tiled=True)]
    unnamed x10 -> x3, waiting for transfers between devices: 151 us -> 0.71 us
    ppermute x0 -> x43, waiting for transfers between devices: none -> 150 us  [the longest x2 44.4 us: owners_sum(): value = kept + lax.ppermute(away, 'ctx', pairs)]
    all_gather x3 -> x2, waiting for transfers between devices: 175 us -> 42.6 us  [gather_all(): whole = lax.all_gather(shard, ('ctx', 'dp'), axis=0, tiled=True)]
    dot_general x19 -> x8, matrix products: 123 us -> 24.3 us  [ein(): return jnp.einsum(form, left, right, preferred_element_type=F32)]
    pallas_call x0 -> x4, Pallas kernels: none -> 95.1 us  [the longest x1 76.4 us: feed_forward(): pl.pallas_call(functools.partial(ffn_kernel, nf), grid=(parts,), in_specs...]
    reduce_scatter x1 -> x0, waiting for transfers between devices: 87.2 us -> none  [body(): lax.psum_scatter(dkv, 'ctx', scatter_dimension=0, tiled=True).astype(F32)]
    ppermute x0 -> x43, starting transfers between devices: none -> 77.5 us  [the longest x2 23.4 us: owners_sum(): value = kept + lax.ppermute(away, 'ctx', pairs)]
  transfers between devices with their start and end apart: 8 -> 46, of which waited for: 8 -> 23; matrix products, arithmetic and copies ran while one was open for 12% -> 22% of each run, Pallas kernels for 2% -> 10%
where the time goes in v2:
time: 614 us; the launch traced here: 605 us
  waiting for transfers between devices  193 us (31%)
  Pallas kernels  141 us (23%)
  local copies, waits for them, and re-layouts  89.5 us (15%)
  starting transfers between devices  77.8 us (13%)
  other arithmetic  63.6 us (10%)
  matrix products  24.3 us (4%)
  between operations  15.1 us (2%)
    pallas_call x1, Pallas kernels, feed_forward(): pl.pallas_call(functools.partial(ffn_kernel, nf), grid=(parts,), in_specs...  76.4 us
    ppermute x2, waiting for transfers between devices, owners_sum(): value = kept + lax.ppermute(away, 'ctx', pairs)  44.4 us
    all_gather x2, waiting for transfers between devices, gather_all(): whole = lax.all_gather(shard, ('ctx', 'dp'), axis=0, tiled=True)  42.6 us
    ppermute x20, waiting for transfers between devices, halve(): return kept + lax.ppermute(away, place[0], partners(*place))  33.3 us
    pallas_call x1, Pallas kernels, attend_back(): pl.pallas_call(functools.partial(back_kernel, heads, size), grid_spec=plt...  26.7 us
    ppermute x10, waiting for transfers between devices, gather_doubling(): other = lax.ppermute(value, place[0], partners(*place))  26.3 us
    dot_general x8, matrix products, ein(): return jnp.einsum(form, left, right, preferred_element_type=F32)  24.3 us
    ppermute x2, waiting for transfers between devices, earlier_blocks(): other = lax.ppermute(value, 'ctx', pairs)  23.8 us
  transfers between devices with their start and end apart: 46, of which 23 were waited for; matrix products, arithmetic and copies ran while one was open for 22% of the time, Pallas kernels for 10%

profile of v2, /device:TPU:0, one launch (start us, length us, event | category | flops | bytes accessed | tf_op | source)
XLA Modules:
  0.0 604.6 jit_solution(9184594181986498688)
XLA Ops:
  40.3 6.6 %collective-permute-done.7 = bf16[2,2,2,120,160]{3,4,1,2,0:T(8,128)(2,1)S(1)} collective-permute-done((bf16[2,2,2,120,160]{3,4,1,2,0:T(8,128)(2,1)S(1)}, bf16[2,2,2,120,160]{3,4,1,2,0:T(8,128)(2,1)S(1)}, u32[]{:S(2)}, u32[]{:S(2)}) %collective-permute-start.7) | collective-permute-done | bytes 307232 | tf_op jit(solution)/shard_map/ppermute | solution.py:208
  47.3 8.1 %collective-permute-done.13 = bf16[2,2,2,120,240]{4,3,2,1,0:T(8,128)(2,1)S(1)} collective-permute-done((bf16[2,2,2,120,240]{4,3,2,1,0:T(8,128)(2,1)}, bf16[2,2,2,120,240]{4,3,2,1,0:T(8,128)(2,1)S(1)}, u32[]{:S(2)}, u32[]{:S(2)}) %collective-permute-start.13) | collective-permute-done | bytes 460832 | tf_op jit(solution)/shard_map/ppermute | solution.py:208
  76.0 23.8 %collective-permute-done.9 = bf16[2,2,640,256]{3,2,1,0:T(8,128)(2,1)} collective-permute-done((bf16[2,2,640,256]{3,2,1,0:T(8,128)(2,1)}, bf16[2,2,640,256]{3,2,1,0:T(8,128)(2,1)}, u32[]{:S(2)}, u32[]{:S(2)}) %collective-permute-start.9) | collective-permute-done | bytes 1310752 | tf_op jit(solution)/shard_map/ppermute | solution.py:245
  133.0 19.3 %attend.1 = (bf16[2,960,512]{2,1,0:T(8,128)(2,1)S(1)}, f32[2,5,3,512]{3,2,1,0:T(4,128)S(1)}) custom-call(s32[12]{0:T(128)S(1)} %reshape.257.bounds, bf16[2,960,512]{2,1,0:T(8,128)(2,1)S(1)} %bitcast.286, bf16[8,2,2,5,64,256]{5,4,3,2,1,0:T(8,128)(2,1)S(1)} %bitcast.285, s32[2,2,512]{2,1,0:T(2,128)S(1)} %pad_add_fusion.2.rows_ref), custom_call_target="tpu_custom_call" | custom-call | flops 6039797760 | bytes 8388608 | tf_op jit(solution)/shard_map/attend/pallas_call | solution.py:134
  153.6 42.6 %all-gather.5.cloned.1.call-done = bf16[3840,1520]{1,0:T(8,128)(2,1)} async-done(((bf16[120,1520]{1,0:T(8,128)(2,1)}), bf16[3840,1520]{1,0:T(8,128)(2,1)}) %all-gather.5.cloned.1.call-update) | async-done | bytes 11673616 | tf_op jit(solution)/shard_map/all_gather | solution.py:167
  203.0 6.9 %multiply_reduce_fusion.2 = (f32[2,512]{1,0:T(2,128)S(1)}, f32[2,512,960]{1,2,0:T(8,128)}) fusion(bf16[960,960,1]{0,1,2:T(8,128)(2,1)} %bitcast.321, bf16[2,960,512]{2,1,0:T(8,128)(2,1)} %copy-done.1, bf16[2,512,960]{1,2,0:T(8,128)(2,1)} %param.12), kind=kOutput, calls=%fused_computation.23 | convolution fusion | flops 1891367936 | bytes 9711616 | tf_op jit(solution)/shard_map/sfc,fd->scd/dot_general | solution.py:413
  209.9 5.2 copy.130
  223.0 76.4 %feed_forward.1 = (bf16[1024,960]{1,0:T(8,128)(2,1)}, f32[1024,960]{1,0:T(8,128)}, bf16[4,960,1280]{2,1,0:T(8,128)(2,1)}, bf16[4,2560,240]{2,1,0:T(8,128)(2,1)}) custom-call(bf16[1024,960]{1,0:T(8,128)(2,1)} %copy.110.h_ref, bf16[960,1024]{1,0:T(8,128)(2,1)} %bitcast.302, bf16[1024,960]{1,0:T(8,128)(2,1)} %bitcast.318, f32[1024,960]{1,0:T(8,128)} %bitcast.308, ...), custom_call_target="tpu_custom_call" | custom-call | flops 45298483200 | bytes 62914560 | tf_op jit(solution)/shard_map/feed_forward/pallas_call | solution.py:375
  306.0 5.4 copy.113
  311.4 5.0 multiply_reduce_fusion
  317.7 5.5 fusion.32
  329.6 26.7 %attend_back.1 = (bf16[2,960,512]{2,1,0:T(8,128)(2,1)S(1)}, bf16[8,2,2,5,64,256]{5,4,3,2,1,0:T(8,128)(2,1)S(1)}) custom-call(s32[12]{0:T(128)S(1)} %reshape.257.bounds, bf16[2,960,512]{2,1,0:T(8,128)(2,1)S(1)} %bitcast.287, bf16[8,2,2,5,64,256]{5,4,3,2,1,0:T(8,128)(2,1)} %bitcast.284, s32[2,2,512]{2,1,0:T(2,128)S(1)} %pad_add_fusion.2.rows_ref, ...), custom_call_target="tpu_custom_call" | custom-call | flops 983040 | bytes 1048576 | tf_op jit(solution)/shard_map/attend_back/pallas_call | solution.py:150
  360.9 22.1 %collective-permute-start.17 = (bf16[2,2,2,640,256]{4,3,2,1,0:T(8,128)(2,1)}, bf16[2,2,2,640,256]{4,3,2,1,0:T(8,128)(2,1)}, u32[]{:S(2)}, u32[]{:S(2)}) collective-permute-start(bf16[2,2,2,640,256]{4,3,2,1,0:T(8,128)(2,1)} %dynamic-slice_bitcast_fusion), channel_id=1, source_target_pairs={{0,1},{1,0},{2,3},{3,2},{4,5},{5,4},{6,7},{7,6},{8,9},{9,8},{10,11... | collective-permute-start | bytes 7864328 | tf_op jit(solution)/shard_map/ppermute | solution.py:263
  384.6 6.5 %weight_term.5 = bf16[4,960,240]{2,1,0:T(8,128)(2,1)S(1)} custom-call(bf16[2,960,512]{2,1,0:T(8,128)(2,1)S(1)} %copy-done.3, bf16[2,4,240,512]{3,2,1,0:T(8,128)(2,1)S(1)} %bitcast.288), custom_call_target="tpu_custom_call" | custom-call | flops 1966080 | bytes 1048576 | tf_op jit(solution)/shard_map/weight_term/pallas_call | solution.py:301
  396.2 6.5 %weight_term.3 = bf16[4,960,240]{2,1,0:T(8,128)(2,1)S(1)} custom-call(bf16[2,960,512]{2,1,0:T(8,128)(2,1)S(1)} %fusion.26.left_ref, bf16[2,4,240,512]{3,2,1,0:T(8,128)(2,1)S(1)} %bitcast.296), custom_call_target="tpu_custom_call" | custom-call | flops 1966080 | bytes 1048576 | tf_op jit(solution)/shard_map/weight_term/pallas_call | solution.py:301
  416.2 5.8 fusion.38
  423.5 44.4 %collective-permute-done.18 = bf16[2,2,640,256]{3,0,2,1:T(2,128)(2,1)} collective-permute-done((bf16[2,2,640,256]{3,0,2,1:T(2,128)(2,1)}, bf16[2,2,640,256]{3,0,2,1:T(2,128)(2,1)}, u32[]{:S(2)}, u32[]{:S(2)}) %collective-permute-start.18) | collective-permute-done | bytes 1310752 | tf_op jit(solution)/shard_map/ppermute | solution.py:263
  487.4 5.7 weight_term.4
  498.0 10.9 %collective-permute-start.24 = (f32[2,960]{1,0:T(2,128)S(1)}, f32[2,960]{1,0:T(2,128)S(1)}, u32[]{:S(2)}, u32[]{:S(2)}) collective-permute-start(f32[2,960]{1,0:T(2,128)S(1)} %add.259), channel_id=1, source_target_pairs={{0,16},{4,20},{8,24},{12,28},{16,0},{20,4},{24,8},{28,12},{1,17},{... | collective-permute-start | bytes 23048 | tf_op jit(solution)/shard_map/ppermute | solution.py:279
  518.5 16.9 %collective-permute-done.26 = f32[2,960]{1,0:T(2,128)S(1)} collective-permute-done((f32[2,960]{1,0:T(2,128)S(1)}, f32[2,960]{1,0:T(2,128)S(1)}, u32[]{:S(2)}, u32[]{:S(2)}) %collective-permute-start.26) | collective-permute-done | bytes 7712 | tf_op jit(solution)/shard_map/ppermute | solution.py:279
  541.5 11.6 %collective-permute-start.29 = (bf16[120,240]{1,0:T(8,128)(2,1)S(1)}, bf16[120,240]{1,0:T(8,128)(2,1)S(1)}, u32[]{:S(2)}, u32[]{:S(2)}) collective-permute-start(bf16[120,240]{1,0:T(8,128)(2,1)S(1)} %dynamic-slice_bitcast_fusion.15), channel_id=1, source_target_pairs={{0,16},{4,20},{8,24},{12,28},{16,0},{20,4},{24,8},{28,12},{1,17},{... | collective-permute-start | bytes 172808 | tf_op jit(solution)/shard_map/ppermute | solution.py:220
  573.4 5.3 collective-permute-done.33
  583.7 5.7 collective-permute-done.41
  591.2 5.9 collective-permute-done.42
  (325 shorter events, 210.8 us)
Async XLA Ops:
  7.2 123.0 %all-gather.3.cloned.1.call-start = ((), (), s32[]{:S(2)}) async-start(), calls=%async_computation.1 | async-start | bytes 5406720 | tf_op jit(solution)/shard_map/all_gather | solution.py:167
  7.9 188.3 %all-gather.5.cloned.1.call-start = ((), (), s32[]{:S(2)}) async-start(), calls=%async_computation.2 | async-start | bytes 12165120 | tf_op jit(solution)/shard_map/all_gather | solution.py:167
  8.0 14.7 %collective-permute-start.10 = (bf16[120,240]{1,0:T(8,128)(2,1)}, bf16[120,240]{1,0:T(8,128)(2,1)S(1)}, u32[]{:S(2)}, u32[]{:S(2)}) collective-permute-start(bf16[120,240]{1,0:T(8,128)(2,1)} %param.16), channel_id=1, source_target_pairs={{0,16},{4,20},{8,24},{12,28},{16,0},{20,4},{24,8},{28,12},{1,17},{... | collective-permute-start | bytes 172808 | tf_op jit(solution)/shard_map/ppermute | solution.py:208
  32.9 13.9 %collective-permute-start.7 = (bf16[2,2,2,120,160]{3,4,1,2,0:T(8,128)(2,1)S(1)}, bf16[2,2,2,120,160]{3,4,1,2,0:T(8,128)(2,1)S(1)}, u32[]{:S(2)}, u32[]{:S(2)}) collective-permute-start(bf16[2,2,2,120,160]{3,4,1,2,0:T(8,128)(2,1)S(1)} %pad_maximum_fusion.12), channel_id=1, source_target_pairs={{0,4},{4,0},{8,12},{12,8},{16,20},{20,16},{24,28},{28,24},{1,5},{5... | collective-permute-start | bytes 921608 | tf_op jit(solution)/shard_map/ppermute | solution.py:208
  39.5 15.9 %collective-permute-start.13 = (bf16[2,2,2,120,240]{4,3,2,1,0:T(8,128)(2,1)}, bf16[2,2,2,120,240]{4,3,2,1,0:T(8,128)(2,1)S(1)}, u32[]{:S(2)}, u32[]{:S(2)}) collective-permute-start(bf16[2,2,2,120,240]{4,3,2,1,0:T(8,128)(2,1)} %pad_maximum_fusion.10), channel_id=1, source_target_pairs={{0,2},{1,3},{2,0},{3,1},{4,6},{5,7},{6,4},{7,5},{8,10},{9,11},{10,... | collective-permute-start | bytes 1382408 | tf_op jit(solution)/shard_map/ppermute | solution.py:208
  47.1 10.4 %collective-permute-start.8 = (bf16[2,2,2,2,120,160]{4,5,1,2,0,3:T(8,128)(2,1)S(1)}, bf16[2,2,2,2,120,160]{4,5,1,2,0,3:T(8,128)(2,1)S(1)}, u32[]{:S(2)}, u32[]{:S(2)}) collective-permute-start(bf16[2,2,2,2,120,160]{4,5,1,2,0,3:T(8,128)(2,1)S(1)} %pad_maximum_fusion.8), channel_id=1, source_target_pairs={{0,1},{1,0},{2,3},{3,2},{4,5},{5,4},{6,7},{7,6},{8,9},{9,8},{10,11... | collective-permute-start | bytes 1843208 | tf_op jit(solution)/shard_map/ppermute | solution.py:208
  57.4 15.2 %collective-permute-start.14 = (bf16[2,2,2,2,120,240]{5,4,3,2,1,0:T(8,128)(2,1)}, bf16[2,2,2,2,120,240]{5,4,3,2,1,0:T(8,128)(2,1)}, u32[]{:S(2)}, u32[]{:S(2)}) collective-permute-start(bf16[2,2,2,2,120,240]{5,4,3,2,1,0:T(8,128)(2,1)} %pad_maximum_fusion.7), channel_id=1, source_target_pairs={{0,1},{1,0},{2,3},{3,2},{4,5},{5,4},{6,7},{7,6},{8,9},{9,8},{10,11... | collective-permute-start | bytes 2764808 | tf_op jit(solution)/shard_map/ppermute | solution.py:208
  68.8 31.0 %collective-permute-start.9 = (bf16[2,2,640,256]{3,2,1,0:T(8,128)(2,1)}, bf16[2,2,640,256]{3,2,1,0:T(8,128)(2,1)}, u32[]{:S(2)}, u32[]{:S(2)}) collective-permute-start(bf16[2,2,640,256]{3,2,1,0:T(8,128)(2,1)} %bitcast.280), channel_id=1, source_target_pairs={{0,2},{1,3},{4,6},{5,7},{8,10},{9,11},{12,14},{13,15},{16,18},{17,... | collective-permute-start | bytes 3932168 | tf_op jit(solution)/shard_map/ppermute | solution.py:245
  99.8 385.8 %reduce-scatter.2.cloned.1.call-start = ((), (), s32[]{:S(2)}) async-start(), calls=%async_computation.3 | async-start | bytes 10137600 | tf_op jit(solution)/shard_map/reduce_scatter | solution.py:173
  106.8 17.0 %collective-permute-start.15 = (bf16[2,2,2,640,256]{4,3,2,1,0:T(8,128)(2,1)}, bf16[2,2,2,640,256]{4,3,2,1,0:T(8,128)(2,1)}, u32[]{:S(2)}, u32[]{:S(2)}) collective-permute-start(bf16[2,2,2,640,256]{4,3,2,1,0:T(8,128)(2,1)} %pad_maximum_fusion.1), channel_id=1, source_target_pairs={{0,1},{1,0},{2,3},{3,2},{4,5},{5,4},{6,7},{7,6},{8,9},{9,8},{10,11... | collective-permute-start | bytes 7864328 | tf_op jit(solution)/shard_map/ppermute | solution.py:245
  305.7 19.8 %collective-permute-start.16 = (bf16[2,2,2,2,320,240]{5,4,2,1,0,3:T(8,128)(2,1)}, bf16[2,2,2,2,320,240]{5,4,2,1,0,3:T(8,128)(2,1)}, u32[]{:S(2)}, u32[]{:S(2)}) collective-permute-start(bf16[2,2,2,2,320,240]{5,4,2,1,0,3:T(8,128)(2,1)} %bitcast.278), channel_id=1, source_target_pairs={{0,1},{1,0},{2,3},{3,2},{4,5},{5,4},{6,7},{7,6},{8,9},{9,8},{10,11... | collective-permute-start | bytes 7372808 | tf_op jit(solution)/shard_map/ppermute | solution.py:220
  360.9 33.0 %collective-permute-start.17 = (bf16[2,2,2,640,256]{4,3,2,1,0:T(8,128)(2,1)}, bf16[2,2,2,640,256]{4,3,2,1,0:T(8,128)(2,1)}, u32[]{:S(2)}, u32[]{:S(2)}) collective-permute-start(bf16[2,2,2,640,256]{4,3,2,1,0:T(8,128)(2,1)} %dynamic-slice_bitcast_fusion), channel_id=1, source_target_pairs={{0,1},{1,0},{2,3},{3,2},{4,5},{5,4},{6,7},{7,6},{8,9},{9,8},{10,11... | collective-permute-start | bytes 7864328 | tf_op jit(solution)/shard_map/ppermute | solution.py:263
  393.3 20.1 %collective-permute-start.21 = (bf16[2,2,2,2,120,240]{5,4,2,1,0,3:T(8,128)(2,1)}, bf16[2,2,2,2,120,240]{5,4,2,1,0,3:T(8,128)(2,1)}, u32[]{:S(2)}, u32[]{:S(2)}) collective-permute-start(bf16[2,2,2,2,120,240]{5,4,2,1,0,3:T(8,128)(2,1)} %bitcast.282), channel_id=1, source_target_pairs={{0,1},{1,0},{2,3},{3,2},{4,5},{5,4},{6,7},{7,6},{8,9},{9,8},{10,11... | collective-permute-start | bytes 2764808 | tf_op jit(solution)/shard_map/ppermute | solution.py:220
  404.9 17.1 %collective-permute-start.19 = (bf16[2,2,2,2,120,240]{5,4,2,1,0,3:T(8,128)(2,1)}, bf16[2,2,2,2,120,240]{5,4,2,1,0,3:T(8,128)(2,1)}, u32[]{:S(2)}, u32[]{:S(2)}) collective-permute-start(bf16[2,2,2,2,120,240]{5,4,2,1,0,3:T(8,128)(2,1)} %bitcast.283), channel_id=1, source_target_pairs={{0,1},{1,0},{2,3},{3,2},{4,5},{5,4},{6,7},{7,6},{8,9},{9,8},{10,11... | collective-permute-start | bytes 2764808 | tf_op jit(solution)/shard_map/ppermute | solution.py:220
  408.0 59.8 %collective-permute-start.18 = (bf16[2,2,640,256]{3,0,2,1:T(2,128)(2,1)}, bf16[2,2,640,256]{3,0,2,1:T(2,128)(2,1)}, u32[]{:S(2)}, u32[]{:S(2)}) collective-permute-start(bf16[2,2,640,256]{3,0,2,1:T(2,128)(2,1)} %bitcast.281), channel_id=1, source_target_pairs={{2,0},{3,1},{6,4},{7,5},{10,8},{11,9},{14,12},{15,13},{18,16},{19,... | collective-permute-start | bytes 3932168 | tf_op jit(solution)/shard_map/ppermute | solution.py:263
  423.4 48.5 %collective-permute-start.20 = (bf16[2,2,2,120,240]{4,3,2,1,0:T(8,128)(2,1)S(1)}, bf16[2,2,2,120,240]{4,3,2,1,0:T(8,128)(2,1)S(1)}, u32[]{:S(2)}, u32[]{:S(2)}) collective-permute-start(bf16[2,2,2,120,240]{4,3,2,1,0:T(8,128)(2,1)S(1)} %dynamic-slice_bitcast_fusion.4), channel_id=1, source_target_pairs={{0,4},{4,0},{8,12},{12,8},{16,20},{20,16},{24,28},{28,24},{1,5},{5... | collective-permute-start | bytes 1382408 | tf_op jit(solution)/shard_map/ppermute | solution.py:220
  494.4 73.7 %collective-permute-start.39 = (bf16[2,2,2,320,240]{4,3,2,1,0:T(8,128)(2,1)}, bf16[2,2,2,320,240]{4,3,2,1,0:T(8,128)(2,1)}, u32[]{:S(2)}, u32[]{:S(2)}) collective-permute-start(bf16[2,2,2,320,240]{4,3,2,1,0:T(8,128)(2,1)} %dynamic-slice_bitcast_fusion.1), channel_id=1, source_target_pairs={{0,4},{4,0},{8,12},{12,8},{16,20},{20,16},{24,28},{28,24},{1,5},{5... | collective-permute-start | bytes 3686408 | tf_op jit(solution)/shard_map/ppermute | solution.py:220
  497.7 55.5 %collective-permute-start.35 = (bf16[2,2,2,120,240]{4,3,2,1,0:T(8,128)(2,1)}, bf16[2,2,2,120,240]{4,3,2,1,0:T(8,128)(2,1)}, u32[]{:S(2)}, u32[]{:S(2)}) collective-permute-start(bf16[2,2,2,120,240]{4,3,2,1,0:T(8,128)(2,1)} %dynamic-slice_bitcast_fusion.3), channel_id=1, source_target_pairs={{0,4},{4,0},{8,12},{12,8},{16,20},{20,16},{24,28},{28,24},{1,5},{5... | collective-permute-start | bytes 1382408 | tf_op jit(solution)/shard_map/ppermute | solution.py:220
  498.0 12.5 %collective-permute-start.24 = (f32[2,960]{1,0:T(2,128)S(1)}, f32[2,960]{1,0:T(2,128)S(1)}, u32[]{:S(2)}, u32[]{:S(2)}) collective-permute-start(f32[2,960]{1,0:T(2,128)S(1)} %add.259), channel_id=1, source_target_pairs={{0,16},{4,20},{8,24},{12,28},{16,0},{20,4},{24,8},{28,12},{1,17},{... | collective-permute-start | bytes 23048 | tf_op jit(solution)/shard_map/ppermute | solution.py:279
  510.5 45.3 %collective-permute-start.30 = (bf16[2,2,2,2,120,160]{4,5,3,2,1,0:T(8,128)(2,1)}, bf16[2,2,2,2,120,160]{4,5,3,2,1,0:T(8,128)(2,1)}, u32[]{:S(2)}, u32[]{:S(2)}) collective-permute-start(bf16[2,2,2,2,120,160]{4,5,3,2,1,0:T(8,128)(2,1)} %bitcast.324), channel_id=1, source_target_pairs={{0,1},{1,0},{2,3},{3,2},{4,5},{5,4},{6,7},{7,6},{8,9},{9,8},{10,11... | collective-permute-start | bytes 1843208 | tf_op jit(solution)/shard_map/ppermute | solution.py:220
  511.6 24.0 %collective-permute-start.27 = (bf16[2,2,120,240]{3,2,1,0:T(8,128)(2,1)S(1)}, bf16[2,2,120,240]{3,2,1,0:T(8,128)(2,1)S(1)}, u32[]{:S(2)}, u32[]{:S(2)}) collective-permute-start(bf16[2,2,120,240]{3,2,1,0:T(8,128)(2,1)S(1)} %dynamic-slice_bitcast_fusion.8), channel_id=1, source_target_pairs={{0,2},{1,3},{2,0},{3,1},{4,6},{5,7},{6,4},{7,5},{8,10},{9,11},{10,... | collective-permute-start | bytes 691208 | tf_op jit(solution)/shard_map/ppermute | solution.py:220
  514.2 21.2 %collective-permute-start.26 = (f32[2,960]{1,0:T(2,128)S(1)}, f32[2,960]{1,0:T(2,128)S(1)}, u32[]{:S(2)}, u32[]{:S(2)}) collective-permute-start(f32[2,960]{1,0:T(2,128)S(1)} %add.261), channel_id=1, source_target_pairs={{0,4},{4,0},{8,12},{12,8},{16,20},{20,16},{24,28},{28,24},{1,5},{5... | collective-permute-start | bytes 23048 | tf_op jit(solution)/shard_map/ppermute | solution.py:279
  541.5 21.1 %collective-permute-start.29 = (bf16[120,240]{1,0:T(8,128)(2,1)S(1)}, bf16[120,240]{1,0:T(8,128)(2,1)S(1)}, u32[]{:S(2)}, u32[]{:S(2)}) collective-permute-start(bf16[120,240]{1,0:T(8,128)(2,1)S(1)} %dynamic-slice_bitcast_fusion.15), channel_id=1, source_target_pairs={{0,16},{4,20},{8,24},{12,28},{16,0},{20,4},{24,8},{28,12},{1,17},{... | collective-permute-start | bytes 172808 | tf_op jit(solution)/shard_map/ppermute | solution.py:220
  569.6 10.8 %collective-permute-start.40 = (bf16[2,2,320,240]{3,2,1,0:T(8,128)(2,1)S(1)}, bf16[2,2,320,240]{3,2,1,0:T(8,128)(2,1)S(1)}, u32[]{:S(2)}, u32[]{:S(2)}) collective-permute-start(bf16[2,2,320,240]{3,2,1,0:T(8,128)(2,1)S(1)} %dynamic-slice_bitcast_fusion.2), channel_id=1, source_target_pairs={{0,2},{1,3},{2,0},{3,1},{4,6},{5,7},{6,4},{7,5},{8,10},{9,11},{10,... | collective-permute-start | bytes 1843208 | tf_op jit(solution)/shard_map/ppermute | solution.py:220
  (64 other events, 329.7 us)
Sparse Core Ops, SparseCore 0:
  10.9 71.3 all-gather.2
  99.9 96.2 all-gather.4
  299.6 142.8 reduce-scatter.1

commit v3 on v2

--- a/solution.py
+++ b/solution.py
@@ -228,12 +228,16 @@
     return value
 
 
+def halve_on(value, flip, begin, end):
+    order = doubling_order(flip)[::-1]
+    left = [place for place in all_places() if place not in order[:begin]]
+    for place in order[begin:end]:
+        value = halve(value, left, place)
+    return value
+
+
 def halve_rest(value, flip, steps):
-    order = doubling_order(flip)[::-1]
-    left = [place for place in all_places() if place not in order[:steps]]
-    for place in order[steps:]:
-        value = halve(value, left, place)
-    return value.astype(F32)
+    return halve_on(value, flip, steps, len(all_places())).astype(F32)
 
 
 def earlier_blocks(own, *later):
@@ -493,7 +497,8 @@
     hidden_one_t = hidden_one.transpose(0, 2, 1)
     dkv, dquery_late = owners_sum(dkv.reshape(parts, tiles, seqs, 2 * heads_kv * HEAD_SIZE, size), dquery)
     query_sum = halve_first(weight_term(hidden_one_t, dquery_late.reshape(seqs, parts, nq, span)), True, 2)
-    dkv, query_sum = lax.optimization_barrier((dkv, query_sum))
+    down_sum, output_sum = halve_on(down_sum, True, 1, 2), halve_on(output_sum, True, 1, 2)
+    dkv, query_sum, down_sum, output_sum = lax.optimization_barrier((dkv, query_sum, down_sum, output_sum))
     dkv = dkv.astype(F32)
     dkv = dkv.transpose(1, 2, 0, 3).reshape(seqs, 2 * heads_kv * HEAD_SIZE, span)
     dkey = rotate_rows(dkv[:, : heads_kv * HEAD_SIZE], cosine, -sine).astype(BF16)
@@ -515,8 +520,8 @@
         (weight_term(hidden_one_t, stacked), query_sum, down_sum, output_sum, jnp.stack([first_term, second_term]))
     )
     query_grad = halve_rest(query_sum, True, 2)
-    down_grad = halve_rest(down_sum, True, 1)
-    output_grad = halve_rest(output_sum, True, 1)
+    down_grad = halve_rest(down_sum, True, 2)
+    output_grad = halve_rest(output_sum, True, 2)
     kv_grads = halve_rest(halve_first(kv_term, False, 1), False, 1)
     key_grad, value_grad = kv_grads[:, :nk], kv_grads[:, nk:]
     input_grad = dafter + dnorm_one

time: 614 us -> 598 us (0.974)
  waiting for transfers between devices: 193 us -> 154 us
  starting transfers between devices: 77.8 us -> 111 us
  local copies, waits for them, and re-layouts: 89.5 us -> 82 us
    ppermute x2, waiting for transfers between devices: 44.4 us -> 13.2 us  [owners_sum(): value = kept + lax.ppermute(away, 'ctx', pairs)]
    ppermute x20, starting transfers between devices: 22.6 us -> 46.1 us  [halve(): return kept + lax.ppermute(away, place[0], partners(*place))]
    ppermute x5, waiting for transfers between devices: 21 us -> 2.59 us  [sum_everywhere(): value = value + lax.ppermute(value, place[0], partners(*place))]
    ppermute x5, starting transfers between devices: 12.8 us -> 26.5 us  [sum_everywhere(): value = value + lax.ppermute(value, place[0], partners(*place))]
    ppermute x20, waiting for transfers between devices: 33.3 us -> 43.9 us  [halve(): return kept + lax.ppermute(away, place[0], partners(*place))]
    unnamed x86 -> x80, local copies, waits for them, and re-layouts: 21.1 us -> 18.9 us
  transfers between devices with their start and end apart: 46 -> 46, of which waited for: 23 -> 24; matrix products, arithmetic and copies ran while one was open for 22% -> 21% of each run, Pallas kernels for 10% -> 10%
where the time goes in v3:
time: 598 us; the launch traced here: 589 us
  waiting for transfers between devices  154 us (26%)
  Pallas kernels  141 us (24%)
  starting transfers between devices  111 us (19%)
  local copies, waits for them, and re-layouts  82 us (14%)
  other arithmetic  63.5 us (11%)
  matrix products  22.7 us (4%)
  between operations  15.3 us (3%)
    pallas_call x1, Pallas kernels, feed_forward(): pl.pallas_call(functools.partial(ffn_kernel, nf), grid=(parts,), in_specs...  76.4 us
    ppermute x20, starting transfers between devices, halve(): return kept + lax.ppermute(away, place[0], partners(*place))  46.1 us
    ppermute x20, waiting for transfers between devices, halve(): return kept + lax.ppermute(away, place[0], partners(*place))  43.9 us
    all_gather x2, waiting for transfers between devices, gather_all(): whole = lax.all_gather(shard, ('ctx', 'dp'), axis=0, tiled=True)  42.4 us
    ppermute x5, starting transfers between devices, sum_everywhere(): value = value + lax.ppermute(value, place[0], partners(*place))  26.5 us
    pallas_call x1, Pallas kernels, attend_back(): pl.pallas_call(functools.partial(back_kernel, heads, size), grid_spec=plt...  26.5 us
    ppermute x10, waiting for transfers between devices, gather_doubling(): other = lax.ppermute(value, place[0], partners(*place))  26.3 us
    ppermute x2, waiting for transfers between devices, earlier_blocks(): other = lax.ppermute(value, 'ctx', pairs)  23.8 us
  transfers between devices with their start and end apart: 46, of which 24 were waited for; matrix products, arithmetic and copies ran while one was open for 21% of the time, Pallas kernels for 10%

profile of v3, /device:TPU:0, one launch (start us, length us, event | category | flops | bytes accessed | tf_op | source)
XLA Modules:
  0.0 589.5 jit_solution(8867971725970628087)
XLA Ops:
  40.3 6.6 %collective-permute-done.7 = bf16[2,2,2,120,160]{3,4,1,2,0:T(8,128)(2,1)S(1)} collective-permute-done((bf16[2,2,2,120,160]{3,4,1,2,0:T(8,128)(2,1)S(1)}, bf16[2,2,2,120,160]{3,4,1,2,0:T(8,128)(2,1)S(1)}, u32[]{:S(2)}, u32[]{:S(2)}) %collective-permute-start.7) | collective-permute-done | bytes 307232 | tf_op jit(solution)/shard_map/ppermute | solution.py:208
  47.3 8.1 %collective-permute-done.13 = bf16[2,2,2,120,240]{4,3,2,1,0:T(8,128)(2,1)S(1)} collective-permute-done((bf16[2,2,2,120,240]{4,3,2,1,0:T(8,128)(2,1)}, bf16[2,2,2,120,240]{4,3,2,1,0:T(8,128)(2,1)S(1)}, u32[]{:S(2)}, u32[]{:S(2)}) %collective-permute-start.13) | collective-permute-done | bytes 460832 | tf_op jit(solution)/shard_map/ppermute | solution.py:208
  60.4 4.7 reshape.258
  76.1 23.7 %collective-permute-done.9 = bf16[2,2,640,256]{3,2,1,0:T(8,128)(2,1)} collective-permute-done((bf16[2,2,640,256]{3,2,1,0:T(8,128)(2,1)}, bf16[2,2,640,256]{3,2,1,0:T(8,128)(2,1)}, u32[]{:S(2)}, u32[]{:S(2)}) %collective-permute-start.9) | collective-permute-done | bytes 1310752 | tf_op jit(solution)/shard_map/ppermute | solution.py:249
  133.2 19.4 %attend.1 = (bf16[2,960,512]{2,1,0:T(8,128)(2,1)S(1)}, f32[2,5,3,512]{3,2,1,0:T(4,128)S(1)}) custom-call(s32[12]{0:T(128)S(1)} %reshape.257.bounds, bf16[2,960,512]{2,1,0:T(8,128)(2,1)S(1)} %bitcast.286, bf16[8,2,2,5,64,256]{5,4,3,2,1,0:T(8,128)(2,1)S(1)} %bitcast.285, s32[2,2,512]{2,1,0:T(2,128)S(1)} %pad_add_fusion.2.rows_ref), custom_call_target="tpu_custom_call" | custom-call | flops 6039797760 | bytes 8388608 | tf_op jit(solution)/shard_map/attend/pallas_call | solution.py:134
  153.8 42.4 %all-gather.5.cloned.1.call-done = bf16[3840,1520]{1,0:T(8,128)(2,1)} async-done(((bf16[120,1520]{1,0:T(8,128)(2,1)}), bf16[3840,1520]{1,0:T(8,128)(2,1)}) %all-gather.5.cloned.1.call-update) | async-done | bytes 11673616 | tf_op jit(solution)/shard_map/all_gather | solution.py:167
  203.0 6.9 %multiply_reduce_fusion.2 = (f32[2,512]{1,0:T(2,128)S(1)}, f32[2,512,960]{1,2,0:T(8,128)}) fusion(bf16[960,960,1]{0,1,2:T(8,128)(2,1)} %bitcast.319, bf16[2,960,512]{2,1,0:T(8,128)(2,1)} %copy-done.1, bf16[2,512,960]{1,2,0:T(8,128)(2,1)} %param.12), kind=kOutput, calls=%fused_computation.23 | convolution fusion | flops 1891367936 | bytes 9711616 | tf_op jit(solution)/shard_map/sfc,fd->scd/dot_general | solution.py:417
  209.9 5.1 copy.130
  222.9 76.4 %feed_forward.1 = (bf16[1024,960]{1,0:T(8,128)(2,1)}, f32[1024,960]{1,0:T(8,128)}, bf16[4,960,1280]{2,1,0:T(8,128)(2,1)}, bf16[4,2560,240]{2,1,0:T(8,128)(2,1)}) custom-call(bf16[1024,960]{1,0:T(8,128)(2,1)} %copy.110.h_ref, bf16[960,1024]{1,0:T(8,128)(2,1)} %bitcast.300, bf16[1024,960]{1,0:T(8,128)(2,1)} %bitcast.316, f32[1024,960]{1,0:T(8,128)} %bitcast.306, ...), custom_call_target="tpu_custom_call" | custom-call | flops 45298483200 | bytes 62914560 | tf_op jit(solution)/shard_map/feed_forward/pallas_call | solution.py:379
  305.9 5.3 copy.113
  311.3 5.0 multiply_reduce_fusion
  317.6 5.6 fusion.32
  329.4 26.5 %attend_back.1 = (bf16[2,960,512]{2,1,0:T(8,128)(2,1)S(1)}, bf16[8,2,2,5,64,256]{5,4,3,2,1,0:T(8,128)(2,1)S(1)}) custom-call(s32[12]{0:T(128)S(1)} %reshape.257.bounds, bf16[2,960,512]{2,1,0:T(8,128)(2,1)S(1)} %bitcast.287, bf16[8,2,2,5,64,256]{5,4,3,2,1,0:T(8,128)(2,1)} %bitcast.284, s32[2,2,512]{2,1,0:T(2,128)S(1)} %pad_add_fusion.2.rows_ref, ...), custom_call_target="tpu_custom_call" | custom-call | flops 983040 | bytes 1048576 | tf_op jit(solution)/shard_map/attend_back/pallas_call | solution.py:150
  360.6 17.8 %collective-permute-start.17 = (bf16[2,2,2,640,256]{4,3,2,1,0:T(8,128)(2,1)}, bf16[2,2,2,640,256]{4,3,2,1,0:T(8,128)(2,1)}, u32[]{:S(2)}, u32[]{:S(2)}) collective-permute-start(bf16[2,2,2,640,256]{4,3,2,1,0:T(8,128)(2,1)} %dynamic-slice_bitcast_fusion), channel_id=1, source_target_pairs={{0,1},{1,0},{2,3},{3,2},{4,5},{5,4},{6,7},{7,6},{8,9},{9,8},{10,11... | collective-permute-start | bytes 7864328 | tf_op jit(solution)/shard_map/ppermute | solution.py:267
  378.5 6.5 %weight_term.4 = bf16[4,960,240]{2,1,0:T(8,128)(2,1)S(1)} custom-call(bf16[2,960,512]{2,1,0:T(8,128)(2,1)S(1)} %copy-done.2, bf16[2,4,240,512]{3,2,1,0:T(8,128)(2,1)S(1)} %bitcast.289), custom_call_target="tpu_custom_call" | custom-call | flops 1966080 | bytes 1048576 | tf_op jit(solution)/shard_map/weight_term/pallas_call | solution.py:305
  393.7 12.2 %collective-permute-start.23 = (bf16[2,2,2,120,240]{4,3,2,1,0:T(8,128)(2,1)S(1)}, bf16[2,2,2,120,240]{4,3,2,1,0:T(8,128)(2,1)S(1)}, u32[]{:S(2)}, u32[]{:S(2)}) collective-permute-start(bf16[2,2,2,120,240]{4,3,2,1,0:T(8,128)(2,1)S(1)} %dynamic-slice_bitcast_fusion.3), channel_id=1, source_target_pairs={{0,4},{4,0},{8,12},{12,8},{16,20},{20,16},{24,28},{28,24},{1,5},{5... | collective-permute-start | bytes 1382408 | tf_op jit(solution)/shard_map/ppermute | solution.py:220
  409.4 6.5 %weight_term.3 = bf16[4,960,240]{2,1,0:T(8,128)(2,1)S(1)} custom-call(bf16[2,960,512]{2,1,0:T(8,128)(2,1)S(1)} %fusion.26.left_ref, bf16[2,4,240,512]{3,2,1,0:T(8,128)(2,1)S(1)} %bitcast.294), custom_call_target="tpu_custom_call" | custom-call | flops 1966080 | bytes 1048576 | tf_op jit(solution)/shard_map/weight_term/pallas_call | solution.py:305
  419.6 6.1 %collective-permute-done.23 = bf16[2,2,2,120,240]{4,3,2,1,0:T(8,128)(2,1)S(1)} collective-permute-done((bf16[2,2,2,120,240]{4,3,2,1,0:T(8,128)(2,1)S(1)}, bf16[2,2,2,120,240]{4,3,2,1,0:T(8,128)(2,1)S(1)}, u32[]{:S(2)}, u32[]{:S(2)}) %collective-permute-start.23) | collective-permute-done | bytes 460832 | tf_op jit(solution)/shard_map/ppermute | solution.py:220
  430.8 25.2 %collective-permute-done.21 = bf16[2,2,2,320,240]{4,3,2,1,0:T(8,128)(2,1)S(1)} collective-permute-done((bf16[2,2,2,320,240]{4,3,2,1,0:T(8,128)(2,1)S(1)}, bf16[2,2,2,320,240]{4,3,2,1,0:T(8,128)(2,1)S(1)}, u32[]{:S(2)}, u32[]{:S(2)}) %collective-permute-start.21) | collective-permute-done | bytes 1228832 | tf_op jit(solution)/shard_map/ppermute | solution.py:220
  457.8 13.2 %collective-permute-done.18 = bf16[2,2,640,256]{3,0,2,1:T(2,128)(2,1)S(1)} collective-permute-done((bf16[2,2,640,256]{3,0,2,1:T(2,128)(2,1)S(1)}, bf16[2,2,640,256]{3,0,2,1:T(2,128)(2,1)S(1)}, u32[]{:S(2)}, u32[]{:S(2)}) %collective-permute-start.18) | collective-permute-done | bytes 1310752 | tf_op jit(solution)/shard_map/ppermute | solution.py:267
  489.4 5.7 weight_term.5
  495.1 11.4 %collective-permute-start.24 = (f32[2,960]{1,0:T(2,128)S(1)}, f32[2,960]{1,0:T(2,128)S(1)}, u32[]{:S(2)}, u32[]{:S(2)}) collective-permute-start(f32[2,960]{1,0:T(2,128)S(1)} %pad_maximum_fusion.17), channel_id=1, source_target_pairs={{0,2},{1,3},{2,0},{3,1},{4,6},{5,7},{6,4},{7,5},{8,10},{9,11},{10,... | collective-permute-start | bytes 23048 | tf_op jit(solution)/shard_map/ppermute | solution.py:283
  515.0 11.5 %collective-permute-start.27 = (f32[2,960]{1,0:T(2,128)S(1)}, f32[2,960]{1,0:T(2,128)S(1)}, u32[]{:S(2)}, u32[]{:S(2)}) collective-permute-start(f32[2,960]{1,0:T(2,128)S(1)} %add.262), channel_id=1, source_target_pairs={{0,8},{4,12},{8,0},{12,4},{16,24},{20,28},{24,16},{28,20},{1,9},{5... | collective-permute-start | bytes 23048 | tf_op jit(solution)/shard_map/ppermute | solution.py:283
  539.7 10.8 %collective-permute-start.39 = (bf16[120,240]{1,0:T(8,128)(2,1)S(1)}, bf16[120,240]{1,0:T(8,128)(2,1)S(1)}, u32[]{:S(2)}, u32[]{:S(2)}) collective-permute-start(bf16[120,240]{1,0:T(8,128)(2,1)S(1)} %dynamic-slice_bitcast_fusion.14), channel_id=1, source_target_pairs={{0,16},{4,20},{8,24},{12,28},{16,0},{20,4},{24,8},{28,12},{1,17},{... | collective-permute-start | bytes 172808 | tf_op jit(solution)/shard_map/ppermute | solution.py:220
  (318 shorter events, 211.5 us)
Async XLA Ops:
  7.2 123.3 %all-gather.3.cloned.1.call-start = ((), (), s32[]{:S(2)}) async-start(), calls=%async_computation.1 | async-start | bytes 5406720 | tf_op jit(solution)/shard_map/all_gather | solution.py:167
  7.9 188.3 %all-gather.5.cloned.1.call-start = ((), (), s32[]{:S(2)}) async-start(), calls=%async_computation.2 | async-start | bytes 12165120 | tf_op jit(solution)/shard_map/all_gather | solution.py:167
  8.0 14.7 %collective-permute-start.10 = (bf16[120,240]{1,0:T(8,128)(2,1)}, bf16[120,240]{1,0:T(8,128)(2,1)S(1)}, u32[]{:S(2)}, u32[]{:S(2)}) collective-permute-start(bf16[120,240]{1,0:T(8,128)(2,1)} %param.16), channel_id=1, source_target_pairs={{0,16},{4,20},{8,24},{12,28},{16,0},{20,4},{24,8},{28,12},{1,17},{... | collective-permute-start | bytes 172808 | tf_op jit(solution)/shard_map/ppermute | solution.py:208
  32.9 13.9 %collective-permute-start.7 = (bf16[2,2,2,120,160]{3,4,1,2,0:T(8,128)(2,1)S(1)}, bf16[2,2,2,120,160]{3,4,1,2,0:T(8,128)(2,1)S(1)}, u32[]{:S(2)}, u32[]{:S(2)}) collective-permute-start(bf16[2,2,2,120,160]{3,4,1,2,0:T(8,128)(2,1)S(1)} %pad_maximum_fusion.12), channel_id=1, source_target_pairs={{0,4},{4,0},{8,12},{12,8},{16,20},{20,16},{24,28},{28,24},{1,5},{5... | collective-permute-start | bytes 921608 | tf_op jit(solution)/shard_map/ppermute | solution.py:208
  39.5 15.9 %collective-permute-start.13 = (bf16[2,2,2,120,240]{4,3,2,1,0:T(8,128)(2,1)}, bf16[2,2,2,120,240]{4,3,2,1,0:T(8,128)(2,1)S(1)}, u32[]{:S(2)}, u32[]{:S(2)}) collective-permute-start(bf16[2,2,2,120,240]{4,3,2,1,0:T(8,128)(2,1)} %pad_maximum_fusion.10), channel_id=1, source_target_pairs={{0,2},{1,3},{2,0},{3,1},{4,6},{5,7},{6,4},{7,5},{8,10},{9,11},{10,... | collective-permute-start | bytes 1382408 | tf_op jit(solution)/shard_map/ppermute | solution.py:208
  47.1 10.4 %collective-permute-start.8 = (bf16[2,2,2,2,120,160]{4,5,1,2,0,3:T(8,128)(2,1)S(1)}, bf16[2,2,2,2,120,160]{4,5,1,2,0,3:T(8,128)(2,1)S(1)}, u32[]{:S(2)}, u32[]{:S(2)}) collective-permute-start(bf16[2,2,2,2,120,160]{4,5,1,2,0,3:T(8,128)(2,1)S(1)} %pad_maximum_fusion.8), channel_id=1, source_target_pairs={{0,1},{1,0},{2,3},{3,2},{4,5},{5,4},{6,7},{7,6},{8,9},{9,8},{10,11... | collective-permute-start | bytes 1843208 | tf_op jit(solution)/shard_map/ppermute | solution.py:208
  57.5 15.2 %collective-permute-start.14 = (bf16[2,2,2,2,120,240]{5,4,3,2,1,0:T(8,128)(2,1)}, bf16[2,2,2,2,120,240]{5,4,3,2,1,0:T(8,128)(2,1)}, u32[]{:S(2)}, u32[]{:S(2)}) collective-permute-start(bf16[2,2,2,2,120,240]{5,4,3,2,1,0:T(8,128)(2,1)} %pad_maximum_fusion.7), channel_id=1, source_target_pairs={{0,1},{1,0},{2,3},{3,2},{4,5},{5,4},{6,7},{7,6},{8,9},{9,8},{10,11... | collective-permute-start | bytes 2764808 | tf_op jit(solution)/shard_map/ppermute | solution.py:208
  68.8 31.0 %collective-permute-start.9 = (bf16[2,2,640,256]{3,2,1,0:T(8,128)(2,1)}, bf16[2,2,640,256]{3,2,1,0:T(8,128)(2,1)}, u32[]{:S(2)}, u32[]{:S(2)}) collective-permute-start(bf16[2,2,640,256]{3,2,1,0:T(8,128)(2,1)} %bitcast.280), channel_id=1, source_target_pairs={{0,2},{1,3},{4,6},{5,7},{8,10},{9,11},{12,14},{13,15},{16,18},{17,... | collective-permute-start | bytes 3932168 | tf_op jit(solution)/shard_map/ppermute | solution.py:249
  99.8 387.7 %reduce-scatter.2.cloned.1.call-start = ((), (), s32[]{:S(2)}) async-start(), calls=%async_computation.3 | async-start | bytes 10137600 | tf_op jit(solution)/shard_map/reduce_scatter | solution.py:173
  107.2 17.0 %collective-permute-start.15 = (bf16[2,2,2,640,256]{4,3,2,1,0:T(8,128)(2,1)}, bf16[2,2,2,640,256]{4,3,2,1,0:T(8,128)(2,1)}, u32[]{:S(2)}, u32[]{:S(2)}) collective-permute-start(bf16[2,2,2,640,256]{4,3,2,1,0:T(8,128)(2,1)} %pad_maximum_fusion.1), channel_id=1, source_target_pairs={{0,1},{1,0},{2,3},{3,2},{4,5},{5,4},{6,7},{7,6},{8,9},{9,8},{10,11... | collective-permute-start | bytes 7864328 | tf_op jit(solution)/shard_map/ppermute | solution.py:249
  305.7 19.8 %collective-permute-start.16 = (bf16[2,2,2,2,320,240]{5,4,2,1,0,3:T(8,128)(2,1)}, bf16[2,2,2,2,320,240]{5,4,2,1,0,3:T(8,128)(2,1)}, u32[]{:S(2)}, u32[]{:S(2)}) collective-permute-start(bf16[2,2,2,2,320,240]{5,4,2,1,0,3:T(8,128)(2,1)} %bitcast.278), channel_id=1, source_target_pairs={{0,1},{1,0},{2,3},{3,2},{4,5},{5,4},{6,7},{7,6},{8,9},{9,8},{10,11... | collective-permute-start | bytes 7372808 | tf_op jit(solution)/shard_map/ppermute | solution.py:220
  360.6 46.0 %collective-permute-start.17 = (bf16[2,2,2,640,256]{4,3,2,1,0:T(8,128)(2,1)}, bf16[2,2,2,640,256]{4,3,2,1,0:T(8,128)(2,1)}, u32[]{:S(2)}, u32[]{:S(2)}) collective-permute-start(bf16[2,2,2,640,256]{4,3,2,1,0:T(8,128)(2,1)} %dynamic-slice_bitcast_fusion), channel_id=1, source_target_pairs={{0,1},{1,0},{2,3},{3,2},{4,5},{5,4},{6,7},{7,6},{8,9},{9,8},{10,11... | collective-permute-start | bytes 7864328 | tf_op jit(solution)/shard_map/ppermute | solution.py:267
  393.7 32.0 %collective-permute-start.23 = (bf16[2,2,2,120,240]{4,3,2,1,0:T(8,128)(2,1)S(1)}, bf16[2,2,2,120,240]{4,3,2,1,0:T(8,128)(2,1)S(1)}, u32[]{:S(2)}, u32[]{:S(2)}) collective-permute-start(bf16[2,2,2,120,240]{4,3,2,1,0:T(8,128)(2,1)S(1)} %dynamic-slice_bitcast_fusion.3), channel_id=1, source_target_pairs={{0,4},{4,0},{8,12},{12,8},{16,20},{20,16},{24,28},{28,24},{1,5},{5... | collective-permute-start | bytes 1382408 | tf_op jit(solution)/shard_map/ppermute | solution.py:220
  406.0 50.0 %collective-permute-start.21 = (bf16[2,2,2,320,240]{4,3,2,1,0:T(8,128)(2,1)S(1)}, bf16[2,2,2,320,240]{4,3,2,1,0:T(8,128)(2,1)S(1)}, u32[]{:S(2)}, u32[]{:S(2)}) collective-permute-start(bf16[2,2,2,320,240]{4,3,2,1,0:T(8,128)(2,1)S(1)} %dynamic-slice_bitcast_fusion.1), channel_id=1, source_target_pairs={{0,4},{4,0},{8,12},{12,8},{16,20},{20,16},{24,28},{28,24},{1,5},{5... | collective-permute-start | bytes 3686408 | tf_op jit(solution)/shard_map/ppermute | solution.py:220
  416.2 41.1 %collective-permute-start.19 = (bf16[2,2,2,2,120,240]{5,4,2,1,0,3:T(8,128)(2,1)S(1)}, bf16[2,2,2,2,120,240]{5,4,2,1,0,3:T(8,128)(2,1)S(1)}, u32[]{:S(2)}, u32[]{:S(2)}) collective-permute-start(bf16[2,2,2,2,120,240]{5,4,2,1,0,3:T(8,128)(2,1)S(1)} %bitcast.323), channel_id=1, source_target_pairs={{0,1},{1,0},{2,3},{3,2},{4,5},{5,4},{6,7},{7,6},{8,9},{9,8},{10,11... | collective-permute-start | bytes 2764808 | tf_op jit(solution)/shard_map/ppermute | solution.py:220
  418.3 52.7 %collective-permute-start.18 = (bf16[2,2,640,256]{3,0,2,1:T(2,128)(2,1)S(1)}, bf16[2,2,640,256]{3,0,2,1:T(2,128)(2,1)S(1)}, u32[]{:S(2)}, u32[]{:S(2)}) collective-permute-start(bf16[2,2,640,256]{3,0,2,1:T(2,128)(2,1)S(1)} %bitcast.321), channel_id=1, source_target_pairs={{2,0},{3,1},{6,4},{7,5},{10,8},{11,9},{14,12},{15,13},{18,16},{19,... | collective-permute-start | bytes 3932168 | tf_op jit(solution)/shard_map/ppermute | solution.py:267
  457.4 16.3 %collective-permute-start.20 = (bf16[2,2,2,120,240]{4,3,2,1,0:T(8,128)(2,1)S(1)}, bf16[2,2,2,120,240]{4,3,2,1,0:T(8,128)(2,1)S(1)}, u32[]{:S(2)}, u32[]{:S(2)}) collective-permute-start(bf16[2,2,2,120,240]{4,3,2,1,0:T(8,128)(2,1)S(1)} %dynamic-slice_bitcast_fusion.4), channel_id=1, source_target_pairs={{0,4},{4,0},{8,12},{12,8},{16,20},{20,16},{24,28},{28,24},{1,5},{5... | collective-permute-start | bytes 1382408 | tf_op jit(solution)/shard_map/ppermute | solution.py:220
  495.1 13.1 %collective-permute-start.24 = (f32[2,960]{1,0:T(2,128)S(1)}, f32[2,960]{1,0:T(2,128)S(1)}, u32[]{:S(2)}, u32[]{:S(2)}) collective-permute-start(f32[2,960]{1,0:T(2,128)S(1)} %pad_maximum_fusion.17), channel_id=1, source_target_pairs={{0,2},{1,3},{2,0},{3,1},{4,6},{5,7},{6,4},{7,5},{8,10},{9,11},{10,... | collective-permute-start | bytes 23048 | tf_op jit(solution)/shard_map/ppermute | solution.py:283
  507.4 50.4 %collective-permute-start.40 = (bf16[2,2,320,240]{3,2,1,0:T(8,128)(2,1)}, bf16[2,2,320,240]{3,2,1,0:T(8,128)(2,1)}, u32[]{:S(2)}, u32[]{:S(2)}) collective-permute-start(bf16[2,2,320,240]{3,2,1,0:T(8,128)(2,1)} %dynamic-slice_bitcast_fusion.2), channel_id=1, source_target_pairs={{0,2},{1,3},{2,0},{3,1},{4,6},{5,7},{6,4},{7,5},{8,10},{9,11},{10,... | collective-permute-start | bytes 1843208 | tf_op jit(solution)/shard_map/ppermute | solution.py:220
  508.2 25.3 %collective-permute-start.37 = (bf16[2,2,120,240]{3,2,1,0:T(8,128)(2,1)S(1)}, bf16[2,2,120,240]{3,2,1,0:T(8,128)(2,1)}, u32[]{:S(2)}, u32[]{:S(2)}) collective-permute-start(bf16[2,2,120,240]{3,2,1,0:T(8,128)(2,1)S(1)} %dynamic-slice_bitcast_fusion.7), channel_id=1, source_target_pairs={{0,2},{1,3},{2,0},{3,1},{4,6},{5,7},{6,4},{7,5},{8,10},{9,11},{10,... | collective-permute-start | bytes 691208 | tf_op jit(solution)/shard_map/ppermute | solution.py:220
  513.6 42.9 %collective-permute-start.32 = (bf16[2,2,2,2,120,160]{4,5,3,2,1,0:T(8,128)(2,1)}, bf16[2,2,2,2,120,160]{4,5,3,2,1,0:T(8,128)(2,1)}, u32[]{:S(2)}, u32[]{:S(2)}) collective-permute-start(bf16[2,2,2,2,120,160]{4,5,3,2,1,0:T(8,128)(2,1)} %bitcast.324), channel_id=1, source_target_pairs={{0,1},{1,0},{2,3},{3,2},{4,5},{5,4},{6,7},{7,6},{8,9},{9,8},{10,11... | collective-permute-start | bytes 1843208 | tf_op jit(solution)/shard_map/ppermute | solution.py:220
  515.0 14.1 %collective-permute-start.27 = (f32[2,960]{1,0:T(2,128)S(1)}, f32[2,960]{1,0:T(2,128)S(1)}, u32[]{:S(2)}, u32[]{:S(2)}) collective-permute-start(f32[2,960]{1,0:T(2,128)S(1)} %add.262), channel_id=1, source_target_pairs={{0,8},{4,12},{8,0},{12,4},{16,24},{20,28},{24,16},{28,20},{1,9},{5... | collective-permute-start | bytes 23048 | tf_op jit(solution)/shard_map/ppermute | solution.py:283
  537.4 13.2 %collective-permute-start.30 = (bf16[2,120,240]{2,1,0:T(8,128)(2,1)S(1)}, bf16[2,120,240]{2,1,0:T(8,128)(2,1)S(1)}, u32[]{:S(2)}, u32[]{:S(2)}) collective-permute-start(bf16[2,120,240]{2,1,0:T(8,128)(2,1)S(1)} %dynamic-slice_bitcast_fusion.12), channel_id=1, source_target_pairs={{0,8},{4,12},{8,0},{12,4},{16,24},{20,28},{24,16},{28,20},{1,9},{5... | collective-permute-start | bytes 345608 | tf_op jit(solution)/shard_map/ppermute | solution.py:220
  539.7 13.0 %collective-permute-start.39 = (bf16[120,240]{1,0:T(8,128)(2,1)S(1)}, bf16[120,240]{1,0:T(8,128)(2,1)S(1)}, u32[]{:S(2)}, u32[]{:S(2)}) collective-permute-start(bf16[120,240]{1,0:T(8,128)(2,1)S(1)} %dynamic-slice_bitcast_fusion.14), channel_id=1, source_target_pairs={{0,16},{4,20},{8,24},{12,28},{16,0},{20,4},{24,8},{28,12},{1,17},{... | collective-permute-start | bytes 172808 | tf_op jit(solution)/shard_map/ppermute | solution.py:220
  (61 other events, 379.3 us)
Sparse Core Ops, SparseCore 0:
  10.9 71.3 all-gather.2
  100.0 96.2 all-gather.4
  299.5 154.8 reduce-scatter.1

commit v4 on v3

--- a/solution.py
+++ b/solution.py
@@ -492,7 +492,7 @@
     output_sum = halve_first(output_term, True, 1)
 
     dattended = ein("fd,scd->sfc", o_full, dattn).astype(BF16)
-    dattended, down_sum = lax.optimization_barrier((dattended, down_sum))
+    dattended, down_sum, output_sum = lax.optimization_barrier((dattended, down_sum, output_sum))
     dquery, dkv = attend_back(query, kv, rows, bounds, attended, dattended, lse, cosine, sine, heads)
     hidden_one_t = hidden_one.transpose(0, 2, 1)
     dkv, dquery_late = owners_sum(dkv.reshape(parts, tiles, seqs, 2 * heads_kv * HEAD_SIZE, size), dquery)

time: 598 us -> 590 us (0.987)
  starting transfers between devices: 111 us -> 97.2 us
  waiting for transfers between devices: 154 us -> 164 us
  other arithmetic: 63.5 us -> 56.2 us
    ppermute x20, starting transfers between devices: 46.1 us -> 32.7 us  [halve(): return kept + lax.ppermute(away, place[0], partners(*place))]
    ppermute x2, waiting for transfers between devices: 13.2 us -> 22.3 us  [owners_sum(): value = kept + lax.ppermute(away, 'ctx', pairs)]
    unnamed x80 -> x82, local copies, waits for them, and re-layouts: 18.9 us -> 21.7 us
  transfers between devices with their start and end apart: 46 -> 46, of which waited for: 24 -> 22; matrix products, arithmetic and copies ran while one was open for 21% -> 20% of each run, Pallas kernels for 10% -> 10%
where the time goes in v4:
time: 590 us; the launch traced here: 582 us
  waiting for transfers between devices  164 us (28%)
  Pallas kernels  141 us (24%)
  starting transfers between devices  97.2 us (16%)
  local copies, waits for them, and re-layouts  85.1 us (14%)
  other arithmetic  56.2 us (10%)
  matrix products  22.7 us (4%)
  between operations  15.3 us (3%)
    pallas_call x1, Pallas kernels, feed_forward(): pl.pallas_call(functools.partial(ffn_kernel, nf), grid=(parts,), in_specs...  76.4 us
    ppermute x20, waiting for transfers between devices, halve(): return kept + lax.ppermute(away, place[0], partners(*place))  45.1 us
    all_gather x2, waiting for transfers between devices, gather_all(): whole = lax.all_gather(shard, ('ctx', 'dp'), axis=0, tiled=True)  42.3 us
    ppermute x20, starting transfers between devices, halve(): return kept + lax.ppermute(away, place[0], partners(*place))  32.7 us
    pallas_call x1, Pallas kernels, attend_back(): pl.pallas_call(functools.partial(back_kernel, heads, size), grid_spec=plt...  26.5 us
    ppermute x10, waiting for transfers between devices, gather_doubling(): other = lax.ppermute(value, place[0], partners(*place))  26.3 us
    ppermute x2, waiting for transfers between devices, earlier_blocks(): other = lax.ppermute(value, 'ctx', pairs)  23.7 us
    ppermute x2, starting transfers between devices, owners_sum(): value = kept + lax.ppermute(away, 'ctx', pairs)  23.5 us
  transfers between devices with their start and end apart: 46, of which 22 were waited for; matrix products, arithmetic and copies ran while one was open for 20% of the time, Pallas kernels for 10%

profile of v4, /device:TPU:0, one launch (start us, length us, event | category | flops | bytes accessed | tf_op | source)
XLA Modules:
  0.0 581.6 jit_solution(551809822882232002)
XLA Ops:
  8.0 4.1 collective-permute-start.10
  23.2 4.1 collective-permute-done.5
  40.3 6.6 %collective-permute-done.7 = bf16[2,2,2,120,160]{3,4,1,2,0:T(8,128)(2,1)S(1)} collective-permute-done((bf16[2,2,2,120,160]{3,4,1,2,0:T(8,128)(2,1)S(1)}, bf16[2,2,2,120,160]{3,4,1,2,0:T(8,128)(2,1)S(1)}, u32[]{:S(2)}, u32[]{:S(2)}) %collective-permute-start.7) | collective-permute-done | bytes 307232 | tf_op jit(solution)/shard_map/ppermute | solution.py:208
  47.3 8.1 %collective-permute-done.13 = bf16[2,2,2,120,240]{4,3,2,1,0:T(8,128)(2,1)S(1)} collective-permute-done((bf16[2,2,2,120,240]{4,3,2,1,0:T(8,128)(2,1)}, bf16[2,2,2,120,240]{4,3,2,1,0:T(8,128)(2,1)S(1)}, u32[]{:S(2)}, u32[]{:S(2)}) %collective-permute-start.13) | collective-permute-done | bytes 460832 | tf_op jit(solution)/shard_map/ppermute | solution.py:208
  60.4 4.7 reshape.258
  76.1 23.7 %collective-permute-done.9 = bf16[2,2,640,256]{3,2,1,0:T(8,128)(2,1)} collective-permute-done((bf16[2,2,640,256]{3,2,1,0:T(8,128)(2,1)}, bf16[2,2,640,256]{3,2,1,0:T(8,128)(2,1)}, u32[]{:S(2)}, u32[]{:S(2)}) %collective-permute-start.9) | collective-permute-done | bytes 1310752 | tf_op jit(solution)/shard_map/ppermute | solution.py:249
  133.2 19.4 %attend.1 = (bf16[2,960,512]{2,1,0:T(8,128)(2,1)S(1)}, f32[2,5,3,512]{3,2,1,0:T(4,128)S(1)}) custom-call(s32[12]{0:T(128)S(1)} %reshape.257.bounds, bf16[2,960,512]{2,1,0:T(8,128)(2,1)S(1)} %bitcast.286, bf16[8,2,2,5,64,256]{5,4,3,2,1,0:T(8,128)(2,1)S(1)} %bitcast.285, s32[2,2,512]{2,1,0:T(2,128)S(1)} %pad_add_fusion.2.rows_ref), custom_call_target="tpu_custom_call" | custom-call | flops 6039797760 | bytes 8388608 | tf_op jit(solution)/shard_map/attend/pallas_call | solution.py:134
  153.9 42.3 %all-gather.5.cloned.1.call-done = bf16[3840,1520]{1,0:T(8,128)(2,1)} async-done(((bf16[120,1520]{1,0:T(8,128)(2,1)}), bf16[3840,1520]{1,0:T(8,128)(2,1)}) %all-gather.5.cloned.1.call-update) | async-done | bytes 11673616 | tf_op jit(solution)/shard_map/all_gather | solution.py:167
  202.9 6.9 %multiply_reduce_fusion.2 = (f32[2,512]{1,0:T(2,128)S(1)}, f32[2,512,960]{1,2,0:T(8,128)}) fusion(bf16[960,960,1]{0,1,2:T(8,128)(2,1)} %bitcast.319, bf16[2,960,512]{2,1,0:T(8,128)(2,1)} %copy-done.1, bf16[2,512,960]{1,2,0:T(8,128)(2,1)} %param.12), kind=kOutput, calls=%fused_computation.23 | convolution fusion | flops 1891367936 | bytes 9711616 | tf_op jit(solution)/shard_map/sfc,fd->scd/dot_general | solution.py:417
  209.8 5.2 copy.130
  222.9 76.4 %feed_forward.1 = (bf16[1024,960]{1,0:T(8,128)(2,1)}, f32[1024,960]{1,0:T(8,128)}, bf16[4,960,1280]{2,1,0:T(8,128)(2,1)}, bf16[4,2560,240]{2,1,0:T(8,128)(2,1)}) custom-call(bf16[1024,960]{1,0:T(8,128)(2,1)} %copy.110.h_ref, bf16[960,1024]{1,0:T(8,128)(2,1)} %bitcast.300, bf16[1024,960]{1,0:T(8,128)(2,1)} %bitcast.316, f32[1024,960]{1,0:T(8,128)} %bitcast.306, ...), custom_call_target="tpu_custom_call" | custom-call | flops 45298483200 | bytes 62914560 | tf_op jit(solution)/shard_map/feed_forward/pallas_call | solution.py:379
  299.4 5.3 copy.113
  304.7 4.5 constant_dynamic-slice_fusion.11
  317.0 6.5 %weight_term.3 = bf16[4,960,240]{2,1,0:T(8,128)(2,1)S(1)} custom-call(bf16[2,960,512]{2,1,0:T(8,128)(2,1)S(1)} %copy-done.2, bf16[2,4,240,512]{3,2,1,0:T(8,128)(2,1)S(1)} %bitcast.289), custom_call_target="tpu_custom_call" | custom-call | flops 1966080 | bytes 1048576 | tf_op jit(solution)/shard_map/weight_term/pallas_call | solution.py:305
  333.1 26.5 %attend_back.1 = (bf16[2,960,512]{2,1,0:T(8,128)(2,1)S(1)}, bf16[8,2,2,5,64,256]{5,4,3,2,1,0:T(8,128)(2,1)S(1)}) custom-call(s32[12]{0:T(128)S(1)} %reshape.257.bounds, bf16[2,960,512]{2,1,0:T(8,128)(2,1)S(1)} %bitcast.287, bf16[8,2,2,5,64,256]{5,4,3,2,1,0:T(8,128)(2,1)} %bitcast.284, s32[2,2,512]{2,1,0:T(2,128)S(1)} %pad_add_fusion.2.rows_ref, ...), custom_call_target="tpu_custom_call" | custom-call | flops 983040 | bytes 1048576 | tf_op jit(solution)/shard_map/attend_back/pallas_call | solution.py:150
  364.1 21.9 %collective-permute-start.18 = (bf16[2,2,2,640,256]{4,3,2,1,0:T(8,128)(2,1)}, bf16[2,2,2,640,256]{4,3,2,1,0:T(8,128)(2,1)}, u32[]{:S(2)}, u32[]{:S(2)}) collective-permute-start(bf16[2,2,2,640,256]{4,3,2,1,0:T(8,128)(2,1)} %dynamic-slice_bitcast_fusion), channel_id=1, source_target_pairs={{0,1},{1,0},{2,3},{3,2},{4,5},{5,4},{6,7},{7,6},{8,9},{9,8},{10,11... | collective-permute-start | bytes 7864328 | tf_op jit(solution)/shard_map/ppermute | solution.py:267
  398.7 6.5 %weight_term.4 = bf16[4,960,240]{2,1,0:T(8,128)(2,1)S(1)} custom-call(bf16[2,960,512]{2,1,0:T(8,128)(2,1)S(1)} %fusion.26.left_ref, bf16[2,4,240,512]{3,2,1,0:T(8,128)(2,1)S(1)} %bitcast.294), custom_call_target="tpu_custom_call" | custom-call | flops 1966080 | bytes 1048576 | tf_op jit(solution)/shard_map/weight_term/pallas_call | solution.py:305
  408.7 4.2 fusion.38
  413.8 30.5 %collective-permute-done.22 = bf16[2,2,2,320,240]{4,3,2,1,0:T(8,128)(2,1)S(1)} collective-permute-done((bf16[2,2,2,320,240]{4,3,2,1,0:T(8,128)(2,1)S(1)}, bf16[2,2,2,320,240]{4,3,2,1,0:T(8,128)(2,1)S(1)}, u32[]{:S(2)}, u32[]{:S(2)}) %collective-permute-start.22) | collective-permute-done | bytes 1228832 | tf_op jit(solution)/shard_map/ppermute | solution.py:220
  447.4 22.3 %collective-permute-done.19 = bf16[2,2,640,256]{3,0,2,1:T(2,128)(2,1)S(1)} collective-permute-done((bf16[2,2,640,256]{3,0,2,1:T(2,128)(2,1)S(1)}, bf16[2,2,640,256]{3,0,2,1:T(2,128)(2,1)S(1)}, u32[]{:S(2)}, u32[]{:S(2)}) %collective-permute-start.19) | collective-permute-done | bytes 1310752 | tf_op jit(solution)/shard_map/ppermute | solution.py:267
  488.2 5.7 weight_term.5
  493.8 6.8 %collective-permute-start.24 = (f32[2,960]{1,0:T(2,128)S(1)}, f32[2,960]{1,0:T(2,128)S(1)}, u32[]{:S(2)}, u32[]{:S(2)}) collective-permute-start(f32[2,960]{1,0:T(2,128)S(1)} %pad_maximum_fusion.17), channel_id=1, source_target_pairs={{0,2},{1,3},{2,0},{3,1},{4,6},{5,7},{6,4},{7,5},{8,10},{9,11},{10,... | collective-permute-start | bytes 23048 | tf_op jit(solution)/shard_map/ppermute | solution.py:283
  504.6 11.3 %collective-permute-start.26 = (f32[2,960]{1,0:T(2,128)S(1)}, f32[2,960]{1,0:T(2,128)S(1)}, u32[]{:S(2)}, u32[]{:S(2)}) collective-permute-start(f32[2,960]{1,0:T(2,128)S(1)} %add.261), channel_id=1, source_target_pairs={{0,16},{4,20},{8,24},{12,28},{16,0},{20,4},{24,8},{28,12},{1,17},{... | collective-permute-start | bytes 23048 | tf_op jit(solution)/shard_map/ppermute | solution.py:283
  533.8 9.8 %collective-permute-start.39 = (bf16[120,240]{1,0:T(8,128)(2,1)S(1)}, bf16[120,240]{1,0:T(8,128)(2,1)S(1)}, u32[]{:S(2)}, u32[]{:S(2)}) collective-permute-start(bf16[120,240]{1,0:T(8,128)(2,1)S(1)} %dynamic-slice_bitcast_fusion.14), channel_id=1, source_target_pairs={{0,16},{4,20},{8,24},{12,28},{16,0},{20,4},{24,8},{28,12},{1,17},{... | collective-permute-start | bytes 172808 | tf_op jit(solution)/shard_map/ppermute | solution.py:220
  (320 shorter events, 203.1 us)
Async XLA Ops:
  7.2 123.2 %all-gather.3.cloned.1.call-start = ((), (), s32[]{:S(2)}) async-start(), calls=%async_computation.1 | async-start | bytes 5406720 | tf_op jit(solution)/shard_map/all_gather | solution.py:167
  7.9 188.3 %all-gather.5.cloned.1.call-start = ((), (), s32[]{:S(2)}) async-start(), calls=%async_computation.2 | async-start | bytes 12165120 | tf_op jit(solution)/shard_map/all_gather | solution.py:167
  8.0 14.7 %collective-permute-start.10 = (bf16[120,240]{1,0:T(8,128)(2,1)}, bf16[120,240]{1,0:T(8,128)(2,1)S(1)}, u32[]{:S(2)}, u32[]{:S(2)}) collective-permute-start(bf16[120,240]{1,0:T(8,128)(2,1)} %param.16), channel_id=1, source_target_pairs={{0,16},{4,20},{8,24},{12,28},{16,0},{20,4},{24,8},{28,12},{1,17},{... | collective-permute-start | bytes 172808 | tf_op jit(solution)/shard_map/ppermute | solution.py:208
  29.7 8.9 %collective-permute-start.12 = (bf16[2,2,120,240]{3,2,1,0:T(8,128)(2,1)S(1)}, bf16[2,2,120,240]{3,2,1,0:T(8,128)(2,1)S(1)}, u32[]{:S(2)}, u32[]{:S(2)}) collective-permute-start(bf16[2,2,120,240]{3,2,1,0:T(8,128)(2,1)S(1)} %pad_maximum_fusion.13), channel_id=1, source_target_pairs={{0,4},{4,0},{8,12},{12,8},{16,20},{20,16},{24,28},{28,24},{1,5},{5... | collective-permute-start | bytes 691208 | tf_op jit(solution)/shard_map/ppermute | solution.py:208
  32.9 13.9 %collective-permute-start.7 = (bf16[2,2,2,120,160]{3,4,1,2,0:T(8,128)(2,1)S(1)}, bf16[2,2,2,120,160]{3,4,1,2,0:T(8,128)(2,1)S(1)}, u32[]{:S(2)}, u32[]{:S(2)}) collective-permute-start(bf16[2,2,2,120,160]{3,4,1,2,0:T(8,128)(2,1)S(1)} %pad_maximum_fusion.12), channel_id=1, source_target_pairs={{0,4},{4,0},{8,12},{12,8},{16,20},{20,16},{24,28},{28,24},{1,5},{5... | collective-permute-start | bytes 921608 | tf_op jit(solution)/shard_map/ppermute | solution.py:208
  39.5 15.9 %collective-permute-start.13 = (bf16[2,2,2,120,240]{4,3,2,1,0:T(8,128)(2,1)}, bf16[2,2,2,120,240]{4,3,2,1,0:T(8,128)(2,1)S(1)}, u32[]{:S(2)}, u32[]{:S(2)}) collective-permute-start(bf16[2,2,2,120,240]{4,3,2,1,0:T(8,128)(2,1)} %pad_maximum_fusion.10), channel_id=1, source_target_pairs={{0,2},{1,3},{2,0},{3,1},{4,6},{5,7},{6,4},{7,5},{8,10},{9,11},{10,... | collective-permute-start | bytes 1382408 | tf_op jit(solution)/shard_map/ppermute | solution.py:208
  47.1 10.4 %collective-permute-start.8 = (bf16[2,2,2,2,120,160]{4,5,1,2,0,3:T(8,128)(2,1)S(1)}, bf16[2,2,2,2,120,160]{4,5,1,2,0,3:T(8,128)(2,1)S(1)}, u32[]{:S(2)}, u32[]{:S(2)}) collective-permute-start(bf16[2,2,2,2,120,160]{4,5,1,2,0,3:T(8,128)(2,1)S(1)} %pad_maximum_fusion.8), channel_id=1, source_target_pairs={{0,1},{1,0},{2,3},{3,2},{4,5},{5,4},{6,7},{7,6},{8,9},{9,8},{10,11... | collective-permute-start | bytes 1843208 | tf_op jit(solution)/shard_map/ppermute | solution.py:208
  57.5 15.2 %collective-permute-start.14 = (bf16[2,2,2,2,120,240]{5,4,3,2,1,0:T(8,128)(2,1)}, bf16[2,2,2,2,120,240]{5,4,3,2,1,0:T(8,128)(2,1)}, u32[]{:S(2)}, u32[]{:S(2)}) collective-permute-start(bf16[2,2,2,2,120,240]{5,4,3,2,1,0:T(8,128)(2,1)} %pad_maximum_fusion.7), channel_id=1, source_target_pairs={{0,1},{1,0},{2,3},{3,2},{4,5},{5,4},{6,7},{7,6},{8,9},{9,8},{10,11... | collective-permute-start | bytes 2764808 | tf_op jit(solution)/shard_map/ppermute | solution.py:208
  68.8 31.0 %collective-permute-start.9 = (bf16[2,2,640,256]{3,2,1,0:T(8,128)(2,1)}, bf16[2,2,640,256]{3,2,1,0:T(8,128)(2,1)}, u32[]{:S(2)}, u32[]{:S(2)}) collective-permute-start(bf16[2,2,640,256]{3,2,1,0:T(8,128)(2,1)} %bitcast.280), channel_id=1, source_target_pairs={{0,2},{1,3},{4,6},{5,7},{8,10},{9,11},{12,14},{13,15},{16,18},{17,... | collective-permute-start | bytes 3932168 | tf_op jit(solution)/shard_map/ppermute | solution.py:249
  99.8 386.5 %reduce-scatter.2.cloned.1.call-start = ((), (), s32[]{:S(2)}) async-start(), calls=%async_computation.3 | async-start | bytes 10137600 | tf_op jit(solution)/shard_map/reduce_scatter | solution.py:173
  107.2 16.9 %collective-permute-start.15 = (bf16[2,2,2,640,256]{4,3,2,1,0:T(8,128)(2,1)}, bf16[2,2,2,640,256]{4,3,2,1,0:T(8,128)(2,1)}, u32[]{:S(2)}, u32[]{:S(2)}) collective-permute-start(bf16[2,2,2,640,256]{4,3,2,1,0:T(8,128)(2,1)} %pad_maximum_fusion.1), channel_id=1, source_target_pairs={{0,1},{1,0},{2,3},{3,2},{4,5},{5,4},{6,7},{7,6},{8,9},{9,8},{10,11... | collective-permute-start | bytes 7864328 | tf_op jit(solution)/shard_map/ppermute | solution.py:249
  311.0 16.6 %collective-permute-start.16 = (bf16[2,2,2,2,320,240]{5,4,2,1,0,3:T(8,128)(2,1)}, bf16[2,2,2,2,320,240]{5,4,2,1,0,3:T(8,128)(2,1)}, u32[]{:S(2)}, u32[]{:S(2)}) collective-permute-start(bf16[2,2,2,2,320,240]{5,4,2,1,0,3:T(8,128)(2,1)} %bitcast.278), channel_id=1, source_target_pairs={{0,1},{1,0},{2,3},{3,2},{4,5},{5,4},{6,7},{7,6},{8,9},{9,8},{10,11... | collective-permute-start | bytes 7372808 | tf_op jit(solution)/shard_map/ppermute | solution.py:220
  364.1 31.5 %collective-permute-start.18 = (bf16[2,2,2,640,256]{4,3,2,1,0:T(8,128)(2,1)}, bf16[2,2,2,640,256]{4,3,2,1,0:T(8,128)(2,1)}, u32[]{:S(2)}, u32[]{:S(2)}) collective-permute-start(bf16[2,2,2,640,256]{4,3,2,1,0:T(8,128)(2,1)} %dynamic-slice_bitcast_fusion), channel_id=1, source_target_pairs={{0,1},{1,0},{2,3},{3,2},{4,5},{5,4},{6,7},{7,6},{8,9},{9,8},{10,11... | collective-permute-start | bytes 7864328 | tf_op jit(solution)/shard_map/ppermute | solution.py:267
  392.0 20.9 %collective-permute-start.23 = (bf16[2,2,2,120,240]{4,3,2,1,0:T(8,128)(2,1)S(1)}, bf16[2,2,2,120,240]{4,3,2,1,0:T(8,128)(2,1)S(1)}, u32[]{:S(2)}, u32[]{:S(2)}) collective-permute-start(bf16[2,2,2,120,240]{4,3,2,1,0:T(8,128)(2,1)S(1)} %dynamic-slice_bitcast_fusion.3), channel_id=1, source_target_pairs={{0,4},{4,0},{8,12},{12,8},{16,20},{20,16},{24,28},{28,24},{1,5},{5... | collective-permute-start | bytes 1382408 | tf_op jit(solution)/shard_map/ppermute | solution.py:220
  395.2 49.0 %collective-permute-start.22 = (bf16[2,2,2,320,240]{4,3,2,1,0:T(8,128)(2,1)S(1)}, bf16[2,2,2,320,240]{4,3,2,1,0:T(8,128)(2,1)S(1)}, u32[]{:S(2)}, u32[]{:S(2)}) collective-permute-start(bf16[2,2,2,320,240]{4,3,2,1,0:T(8,128)(2,1)S(1)} %dynamic-slice_bitcast_fusion.1), channel_id=1, source_target_pairs={{0,4},{4,0},{8,12},{12,8},{16,20},{20,16},{24,28},{28,24},{1,5},{5... | collective-permute-start | bytes 3686408 | tf_op jit(solution)/shard_map/ppermute | solution.py:220
  405.4 40.1 %collective-permute-start.20 = (bf16[2,2,2,2,120,240]{5,4,2,1,0,3:T(8,128)(2,1)S(1)}, bf16[2,2,2,2,120,240]{5,4,2,1,0,3:T(8,128)(2,1)S(1)}, u32[]{:S(2)}, u32[]{:S(2)}) collective-permute-start(bf16[2,2,2,2,120,240]{5,4,2,1,0,3:T(8,128)(2,1)S(1)} %bitcast.323), channel_id=1, source_target_pairs={{0,1},{1,0},{2,3},{3,2},{4,5},{5,4},{6,7},{7,6},{8,9},{9,8},{10,11... | collective-permute-start | bytes 2764808 | tf_op jit(solution)/shard_map/ppermute | solution.py:220
  407.1 62.6 %collective-permute-start.19 = (bf16[2,2,640,256]{3,0,2,1:T(2,128)(2,1)S(1)}, bf16[2,2,640,256]{3,0,2,1:T(2,128)(2,1)S(1)}, u32[]{:S(2)}, u32[]{:S(2)}) collective-permute-start(bf16[2,2,640,256]{3,0,2,1:T(2,128)(2,1)S(1)} %bitcast.321), channel_id=1, source_target_pairs={{2,0},{3,1},{6,4},{7,5},{10,8},{11,9},{14,12},{15,13},{18,16},{19,... | collective-permute-start | bytes 3932168 | tf_op jit(solution)/shard_map/ppermute | solution.py:267
  445.7 26.8 %collective-permute-start.21 = (bf16[2,2,2,120,240]{4,3,2,1,0:T(8,128)(2,1)S(1)}, bf16[2,2,2,120,240]{4,3,2,1,0:T(8,128)(2,1)S(1)}, u32[]{:S(2)}, u32[]{:S(2)}) collective-permute-start(bf16[2,2,2,120,240]{4,3,2,1,0:T(8,128)(2,1)S(1)} %dynamic-slice_bitcast_fusion.4), channel_id=1, source_target_pairs={{0,4},{4,0},{8,12},{12,8},{16,20},{20,16},{24,28},{28,24},{1,5},{5... | collective-permute-start | bytes 1382408 | tf_op jit(solution)/shard_map/ppermute | solution.py:220
  501.5 50.0 %collective-permute-start.40 = (bf16[2,2,320,240]{3,2,1,0:T(8,128)(2,1)}, bf16[2,2,320,240]{3,2,1,0:T(8,128)(2,1)}, u32[]{:S(2)}, u32[]{:S(2)}) collective-permute-start(bf16[2,2,320,240]{3,2,1,0:T(8,128)(2,1)} %dynamic-slice_bitcast_fusion.2), channel_id=1, source_target_pairs={{0,2},{1,3},{2,0},{3,1},{4,6},{5,7},{6,4},{7,5},{8,10},{9,11},{10,... | collective-permute-start | bytes 1843208 | tf_op jit(solution)/shard_map/ppermute | solution.py:220
  502.3 25.3 %collective-permute-start.37 = (bf16[2,2,120,240]{3,2,1,0:T(8,128)(2,1)S(1)}, bf16[2,2,120,240]{3,2,1,0:T(8,128)(2,1)}, u32[]{:S(2)}, u32[]{:S(2)}) collective-permute-start(bf16[2,2,120,240]{3,2,1,0:T(8,128)(2,1)S(1)} %dynamic-slice_bitcast_fusion.7), channel_id=1, source_target_pairs={{0,2},{1,3},{2,0},{3,1},{4,6},{5,7},{6,4},{7,5},{8,10},{9,11},{10,... | collective-permute-start | bytes 691208 | tf_op jit(solution)/shard_map/ppermute | solution.py:220
  504.6 12.9 %collective-permute-start.26 = (f32[2,960]{1,0:T(2,128)S(1)}, f32[2,960]{1,0:T(2,128)S(1)}, u32[]{:S(2)}, u32[]{:S(2)}) collective-permute-start(f32[2,960]{1,0:T(2,128)S(1)} %add.261), channel_id=1, source_target_pairs={{0,16},{4,20},{8,24},{12,28},{16,0},{20,4},{24,8},{28,12},{1,17},{... | collective-permute-start | bytes 23048 | tf_op jit(solution)/shard_map/ppermute | solution.py:283
  517.2 32.3 %collective-permute-start.32 = (bf16[2,2,2,2,120,160]{4,5,3,2,1,0:T(8,128)(2,1)}, bf16[2,2,2,2,120,160]{4,5,3,2,1,0:T(8,128)(2,1)}, u32[]{:S(2)}, u32[]{:S(2)}) collective-permute-start(bf16[2,2,2,2,120,160]{4,5,3,2,1,0:T(8,128)(2,1)} %bitcast.325), channel_id=1, source_target_pairs={{0,1},{1,0},{2,3},{3,2},{4,5},{5,4},{6,7},{7,6},{8,9},{9,8},{10,11... | collective-permute-start | bytes 1843208 | tf_op jit(solution)/shard_map/ppermute | solution.py:220
  531.5 12.1 %collective-permute-start.30 = (bf16[2,120,240]{2,1,0:T(8,128)(2,1)S(1)}, bf16[2,120,240]{2,1,0:T(8,128)(2,1)S(1)}, u32[]{:S(2)}, u32[]{:S(2)}) collective-permute-start(bf16[2,120,240]{2,1,0:T(8,128)(2,1)S(1)} %dynamic-slice_bitcast_fusion.12), channel_id=1, source_target_pairs={{0,8},{4,12},{8,0},{12,4},{16,24},{20,28},{24,16},{28,20},{1,9},{5... | collective-permute-start | bytes 345608 | tf_op jit(solution)/shard_map/ppermute | solution.py:220
  533.8 12.5 %collective-permute-start.39 = (bf16[120,240]{1,0:T(8,128)(2,1)S(1)}, bf16[120,240]{1,0:T(8,128)(2,1)S(1)}, u32[]{:S(2)}, u32[]{:S(2)}) collective-permute-start(bf16[120,240]{1,0:T(8,128)(2,1)S(1)} %dynamic-slice_bitcast_fusion.14), channel_id=1, source_target_pairs={{0,16},{4,20},{8,24},{12,28},{16,0},{20,4},{24,8},{28,12},{1,17},{... | collective-permute-start | bytes 172808 | tf_op jit(solution)/shard_map/ppermute | solution.py:220
  (62 other events, 360.7 us)
Sparse Core Ops, SparseCore 0:
  10.9 71.3 all-gather.2
  100.0 96.1 all-gather.4
  299.5 152.6 reduce-scatter.1
